TPU v7x, 32 devices: a whole 2x2x4 slice. The times are simulated.
32 devices in a mesh: groups: 2 (over x), narrow: 16 (over z, y, core).
Axes of the slice: x: 2, y: 2, z: 4, core: 2. Of those that a mesh axis runs over, the one named last changes fastest.
Arguments:
- modes: bfloat16 [32768, 1024], P(('groups', 'narrow')), parts along dimension 0, may hold values from -6 to 6
- node_index: int32 [3, 65536], P(None, ('groups', 'narrow')), parts along dimension 1, may hold values from 0 to 16383, as said below
- interp_weight: float32 [3, 65536], P(None, ('groups', 'narrow')), parts along dimension 1, may hold values from 0.1 to 1
- leaf_order: int32 [65536], P(('groups', 'narrow')), parts along dimension 0, may hold values from 0 to 2047, as said below
- leaf_inverse: bfloat16 [65536, 2048], P(('groups', 'narrow')), parts along dimension 0
- v_factor: float32 [4, 64, 65536], P(None, None, ('groups', 'narrow')), parts along dimension 2
- u_factor: float32 [4, 64, 65536], P(None, None, ('groups', 'narrow')), parts along dimension 2, may hold values from -0.375 to 0.375
- core_table: float32 [30, 128, 128], P('groups'), parts along dimension 0
- level_rank: int32 [8], P('groups'), parts along dimension 0, may hold values from 16 to 64, as said below
Outputs:
- potential: float32 [65536, 1024], P(('groups', 'narrow')), parts along dimension 0
There are 2 independent parts, one for each index of `groups`. A program takes and returns all parts, laid end to end along the dimension named above; each array names one. Nothing has to cross between parts.
Inputs may be any that keep to these rules, and one draw needn't show every extreme that they name: node_index[j, p] lies between (p // 2048) * 1024 - 128 and (p // 2048 + 1) * 1024 + 127, clipped to the nodes that exist; both ends are reached in every leaf. `leaf_order`: each aligned block of 2048 entries is a permutation of 0 to 2047. `level_rank`: some level has rank 64.
All inputs are finite; a program needn't handle non-finite values.
Results may differ from a plain program's by a relative error of at most 0.0029.
Values may be sent and summed in bfloat16 or wider, within the bound.
No kernel may reach another device: no remote copies, remote signals or barrier semaphores. Data moves between devices by JAX's collectives and lax.ppermute only.
A program may use at most 192 MiB of HBM per device.

v0:
```python
import functools

import jax
import jax.numpy as jnp
from jax import lax
from jax.experimental import pallas as pl
from jax.experimental.pallas import tpu as pltpu
from jax.sharding import PartitionSpec as P

HALO = 128
LANES = 128
F32 = jnp.float32
BF16 = jnp.bfloat16
F8 = jnp.float8_e4m3fn
LOW_SCALE = 4096.0
HIGHEST = lax.Precision.HIGHEST
MIB = 2**20


def whole():
    return pl.BlockSpec(memory_space=pltpu.VMEM)


def anywhere():
    return pl.BlockSpec(memory_space=pl.ANY)


def in_hbm(value):
    return pltpu.with_memory_space_constraint(value, pltpu.HBM)


def scalars():
    return pl.BlockSpec(memory_space=pltpu.SMEM)


def params(mib):
    return pltpu.CompilerParams(vmem_limit_bytes=mib * MIB)


def cost(flops, nbytes):
    return pl.CostEstimate(flops=int(flops), bytes_accessed=int(nbytes), transcendentals=0)


def ceil_to(value, unit):
    return -(-value // unit) * unit


def dot(a, b):
    return jnp.dot(a, b, preferred_element_type=F32)


def dot_nt(a, b):
    return lax.dot_general(a, b, (((1,), (1,)), ((), ())), preferred_element_type=F32)


def split(value):
    high = value.astype(BF16)
    return high, (value - high.astype(F32)).astype(BF16)


def masked_level(ref, rank_ref, level, rank_k):
    rows = ref[level * rank_k : (level + 1) * rank_k, :]
    place = lax.broadcasted_iota(jnp.int32, rows.shape, 0)
    return jnp.where(place < rank_ref[level], rows, 0.0)


def interpolation_matrix(
    device_ref,
    rank_ref,
    order_hbm,
    index_hbm,
    weight_hbm,
    modes_ref,
    core_ref,
    v_hbm,
    a_hbm,
    sh_ref,
    sl_ref,
    s8_ref,
    up_ref,
    down_ref,
    cores_ref,
    vs_ref,
    a_ref,
    order_ref,
    index_ref,
    weight_ref,
    v_ref,
    rows_scr,
    cols_scr,
    sems,
    *,
    levels,
    rank_k,
):
    own = modes_ref.shape[0]
    groups = order_ref.shape[0]
    width = sh_ref.shape[1]
    device = device_ref[0]
    small = [
        pltpu.make_async_copy(order_hbm, order_ref, sems.at[2 + levels]),
        pltpu.make_async_copy(index_hbm, index_ref, sems.at[3 + levels]),
        pltpu.make_async_copy(weight_hbm, weight_ref, sems.at[4 + levels]),
    ]
    v_copy = pltpu.make_async_copy(v_hbm, v_ref, sems.at[5 + levels])
    cut = a_ref.shape[1]
    a_copy = pltpu.make_async_copy(a_hbm.at[:, pl.ds(0, cut)], a_ref, sems.at[6 + levels])
    copies = [
        pltpu.make_async_copy(modes_ref.at[pl.ds(own - HALO, HALO)], up_ref, sems.at[0]),
        pltpu.make_async_copy(modes_ref.at[pl.ds(0, HALO)], down_ref, sems.at[1]),
    ]
    for level in range(levels):
        slot = 2 ** (levels - 1 - level) - 1 + lax.shift_right_logical(device, level + 1)
        copies.append(
            pltpu.make_async_copy(core_ref.at[slot], cores_ref.at[level], sems.at[2 + level])
        )
    for copy in small + copies + [v_copy, a_copy]:
        copy.start()
    for copy in small:
        copy.wait()

    rows_scr[...] = jnp.zeros(rows_scr.shape, F32)
    base = device * own
    for first in range(0, groups, 8):
        order = order_ref[first : first + 8, :]
        row_of = lax.shift_right_logical(order, 7)
        lane_of = jnp.bitwise_and(order, LANES - 1)
        taken = []
        for ref in (index_ref, weight_ref):
            for j in range(3):
                total = jnp.zeros((8, LANES), ref.dtype)
                for r in range(groups):
                    table = jnp.broadcast_to(ref[j : j + 1, r * LANES : (r + 1) * LANES], (8, LANES))
                    got = jnp.take_along_axis(table, lane_of, axis=1)
                    total = jnp.where(row_of == r, got, total)
                taken.append(total)
        cols = []
        for node in taken[:3]:
            node = node - base
            cols.append(
                jnp.where(
                    node < 0, node + (own + HALO), jnp.where(node >= own, node + HALO, node)
                )
            )
        w = taken[3:]
        same = cols[2] == cols[0]
        w[0] = w[0] + jnp.where(same, w[2], 0.0)
        cols[2] = jnp.where(same, -1, cols[2])
        same = cols[2] == cols[1]
        w[1] = w[1] + jnp.where(same, w[2], 0.0)
        cols[2] = jnp.where(same, -1, cols[2])
        same = cols[1] == cols[0]
        w[0] = w[0] + jnp.where(same, w[1], 0.0)
        cols[1] = jnp.where(same, -1, cols[1])
        highs = [x.astype(BF16).astype(F32) for x in w]
        lows = [(x - high) * LOW_SCALE for x, high in zip(w, highs)]
        for quantity, value in enumerate([x.astype(F32) for x in cols] + highs + lows):
            for r in range(8):
                at = r * 16 + quantity
                rows_scr[first // 8, at : at + 1, :] = value[r : r + 1, :]
    for part in range(groups // 8):
        cols_scr[part] = rows_scr[part].T

    lane = lax.broadcasted_iota(jnp.int32, (LANES, LANES), 1).astype(jnp.int16)
    zero = jnp.zeros((LANES, LANES), BF16)

    def build(group, carry):
        part = lax.div(group, 8)
        turn = lax.rem(LANES - (group - part * 8) * 16, LANES)
        columns = pltpu.roll(cols_scr[part], turn, axis=1)

        def spread(j):
            return jnp.broadcast_to(columns[:, j : j + 1], (LANES, LANES))

        index = [spread(j).astype(jnp.int32).astype(jnp.int16) for j in range(3)]
        high = [spread(3 + j).astype(BF16) for j in range(3)]
        low = [spread(6 + j).astype(BF16) for j in range(3)]
        rows = pl.ds(pl.multiple_of(group * LANES, LANES), LANES)
        for first in range(0, width, LANES):
            s_high, s_low = zero, zero
            for j in range(3):
                here = (index[j] - jnp.int16(first)) == lane
                s_high = jnp.where(here, high[j], s_high)
                s_low = jnp.where(here, low[j], s_low)
            sh_ref[rows, first : first + LANES] = s_high
            sl_ref[rows, first : first + LANES] = s_low
            s8_ref[rows, first : first + LANES] = s_low.astype(F8)
        return carry

    lax.fori_loop(0, groups, build, 0)
    v_copy.wait()
    ranks = levels * rank_k
    for level in range(levels):
        high, low = split(masked_level(v_ref, rank_ref, level, rank_k))
        vs_ref[level * rank_k : (level + 1) * rank_k, :] = high
        vs_ref[ranks + level * rank_k : ranks + (level + 1) * rank_k, :] = low
    for copy in copies + [a_copy]:
        copy.wait()


def leaf_operators(
    rank_ref, v_split, u_hbm, a0_ref, a_hbm, w_ref, h_ref, left_ref, a1_ref, u_ref, sems, *, levels, rank_k
):
    ranks = levels * rank_k
    piece = 256
    cut = a0_ref.shape[1]
    pieces = range(0, a1_ref.shape[1], piece)
    copies = [
        pltpu.make_async_copy(
            a_hbm.at[:, pl.ds(cut + first, piece)],
            a1_ref.at[:, pl.ds(first, piece)],
            sems.at[1 + first // piece],
        )
        for first in pieces
    ]
    u_copy = pltpu.make_async_copy(u_hbm, u_ref, sems.at[0])
    for copy in copies + [u_copy]:
        copy.start()

    def product(block, at):
        w = dot(v_split[...], block)
        high, low = split(w[:ranks] + w[ranks:])
        w_ref[:ranks, at : at + piece] = high
        w_ref[ranks:, at : at + piece] = low

    for first in range(0, cut, piece):
        product(a0_ref[:, first : first + piece], first)
    for copy, first in zip(copies, pieces):
        copy.wait()
        product(a1_ref[:, first : first + piece], cut + first)
    u_copy.wait()
    for level in range(levels):
        rows = slice(level * rank_k, (level + 1) * rank_k)
        u_ref[rows, :] = masked_level(u_ref, rank_ref, level, rank_k)
    for position, level in enumerate(range(levels - 2, -1, -1)):
        high, low = split(u_ref[level * rank_k : (level + 1) * rank_k, :])
        part = dot_nt(v_split[...], high)
        part = part[:ranks] + part[ranks:] + dot_nt(v_split[:ranks, :], low)
        h_ref[:, position * rank_k : (position + 1) * rank_k] = part
    used = (levels - 1) * rank_k
    if used < h_ref.shape[1]:
        h_ref[:, used:] = jnp.zeros((ranks, h_ref.shape[1] - used), F32)
    for first in range(0, u_ref.shape[1], piece):
        rows = slice(first, first + piece)
        high, low = split(u_ref[:, rows].T)
        left_ref[rows, :ranks] = high
        left_ref[rows, ranks:] = low


def projections(
    device_ref,
    w_ref,
    sh_ref,
    sl_ref,
    modes_ref,
    low_ref,
    high_ref,
    h_ref,
    keep_ref,
    send_ref,
    m_ref,
    m8_ref,
    ws_scr,
    p_scr,
):
    ranks = keep_ref.shape[0]
    own = modes_ref.shape[0]
    half = modes_ref.shape[1] // 2
    m_ref[:own, :] = modes_ref[...]
    m_ref[own : own + HALO, :] = low_ref[...]
    m_ref[own + HALO :, :] = high_ref[...]
    m8_ref[...] = m_ref[...].astype(F8)
    piece = 256
    for first in range(0, sh_ref.shape[1], piece):
        cols = slice(first, first + piece)
        part = dot(w_ref[...], sh_ref[:, cols])
        part = part[:ranks] + part[ranks:]
        part = part + dot(w_ref[:ranks, :], sl_ref[:, cols]) * (1.0 / LOW_SCALE)
        high, low = split(part)
        ws_scr[:ranks, cols] = high
        ws_scr[ranks:, cols] = low
    for first in range(0, 2 * half, piece):
        cols = slice(first, first + piece)
        part = dot(ws_scr[...], m_ref[:, cols])
        p_scr[:, cols] = part[:ranks] + part[ranks:]
    core = jnp.bitwise_and(device_ref[0], 1)
    mine = pl.multiple_of(core * half, half)
    other = pl.multiple_of((1 - core) * half, half)
    keep_ref[:, :half] = p_scr[:, pl.ds(mine, half)]
    send_ref[:, :half] = p_scr[:, pl.ds(other, half)]
    keep_ref[:, half:] = h_ref[...]
    send_ref[:, half:] = h_ref[...]


def stage(device_ref, core_ref, mine_ref, other_ref, *refs, level, levels, rank_k, half):
    side = jnp.bitwise_and(lax.shift_right_logical(device_ref[0], level), 1)
    upper = jnp.full((rank_k, half), side, jnp.int32) == 1
    mine = mine_ref[:rank_k, :half]
    other = other_ref[:rank_k, :half].astype(F32)
    stack = jnp.concatenate([jnp.where(upper, other, mine), jnp.where(upper, mine, other)], axis=0)
    coef = jnp.dot(core_ref[level], stack, precision=HIGHEST, preferred_element_type=F32)
    c_mine = jnp.where(upper, coef[:rank_k], coef[rank_k:])
    c_other = jnp.where(upper, coef[rank_k:], coef[:rank_k])
    if level < levels - 1:
        next_ref, send_ref, c_ref = refs[0], refs[1], refs[2]
        at = half + (levels - 2 - level) * rank_k
        h_mine = mine_ref[rank_k:, at : at + rank_k]
        h_other = other_ref[rank_k:, at : at + rank_k].astype(F32)
        q = mine_ref[rank_k:, :half] + other_ref[rank_k:, :half].astype(F32)
        q = q - jnp.dot(h_mine, c_mine, precision=HIGHEST, preferred_element_type=F32)
        q = q - jnp.dot(h_other, c_other, precision=HIGHEST, preferred_element_type=F32)
        next_ref[:, :half] = q
        send_ref[:, :half] = q.astype(send_ref.dtype)
        end = next_ref.shape[1]
        if end > half:
            h = mine_ref[rank_k:, half:end] + other_ref[rank_k:, half:end].astype(F32)
            next_ref[:, half:] = h
            send_ref[:, half:] = h.astype(send_ref.dtype)
        c_ref[0] = c_mine
        if level == 0:
            c_ref[1] = c_other
    else:
        before, keep_ref, send_ref = refs[: levels - 1], refs[-2], refs[-1]
        for ref_level, ref in enumerate(before):
            rows = slice(ref_level * rank_k, (ref_level + 1) * rank_k)
            keep_ref[rows, :] = ref[0]
            send_ref[rows, :] = ref[1] if ref_level == 0 else ref[0]
        rows = slice(level * rank_k, (level + 1) * rank_k)
        keep_ref[rows, :] = c_mine
        send_ref[rows, :] = c_other if level == 0 else c_mine


def interpolate(sh_ref, s8_ref, m_ref, m8_ref, t_ref, *, start):
    block, piece = 512, 256
    for row in range(0, t_ref.shape[0], block):
        rows = slice(start + row, start + row + block)
        for first in range(0, t_ref.shape[1], piece):
            cols = slice(first, first + piece)
            part = dot(sh_ref[rows, :], m_ref[:, cols])
            part = part + dot(s8_ref[rows, :], m8_ref[:, cols]) * (1.0 / LOW_SCALE)
            t_ref[row : row + block, cols] = part.astype(BF16)


def leaf_solve(a0_ref, a1_ref, t0_ref, t1_ref, y_ref, *, start):
    block, piece = 512, 256
    for row in range(0, y_ref.shape[0], block):
        rows = slice(start + row, start + row + block)
        for first in range(0, y_ref.shape[1], piece):
            cols = slice(first, first + piece)
            part = dot(a0_ref[rows, :], t0_ref[:, cols]) + dot(a1_ref[rows, :], t1_ref[:, cols])
            y_ref[row : row + block, cols] = part


def update(device_ref, left_ref, y0_ref, y1_ref, keep_ref, got_ref, out_ref, c_scr, o_scr, sems):
    ranks, half = keep_ref.shape
    core = jnp.bitwise_and(device_ref[0], 1)
    mine = pl.multiple_of(core * half, half)
    other = pl.multiple_of((1 - core) * half, half)
    for ref, at in ((keep_ref, mine), (got_ref, other)):
        high, low = split(ref[...])
        c_scr[:ranks, pl.ds(at, half)] = high
        c_scr[ranks : 2 * ranks, pl.ds(at, half)] = high
        c_scr[2 * ranks :, pl.ds(at, half)] = low
    block, piece = 256, 256
    copies = []
    for row in range(0, o_scr.shape[0], block):
        rows = slice(row, row + block)
        if row < y0_ref.shape[0]:
            ref, at = y0_ref, row
        else:
            ref, at = y1_ref, row - y0_ref.shape[0]
        for first in range(0, 2 * half, piece):
            cols = slice(first, first + piece)
            part = dot(left_ref[rows, :], c_scr[: 2 * ranks, cols])
            part = part + dot(left_ref[rows, :ranks], c_scr[2 * ranks :, cols])
            o_scr[rows, cols] = ref[at : at + block, cols] - part
        copy = pltpu.make_async_copy(
            o_scr.at[pl.ds(row, block)], out_ref.at[pl.ds(row, block)], sems.at[row // block]
        )
        copy.start()
        copies.append(copy)
    for copy in copies:
        copy.wait()


def local(
    modes,
    node_index,
    interp_weight,
    leaf_order,
    leaf_inverse,
    v_factor,
    u_factor,
    core_table,
    level_rank,
):
    own, rhs = modes.shape
    half = rhs // 2
    levels, rank_k, leaf = v_factor.shape
    ranks = levels * rank_k
    count = lax.axis_size("narrow")
    device = lax.axis_index("narrow").astype(jnp.int32)
    device = device.reshape(1)
    width = own + 2 * HALO
    shape = pltpu.VMEM
    half_rows = leaf // 2

    def partner(value, bit):
        return lax.ppermute(value, "narrow", [(s, s ^ (1 << bit)) for s in range(count)])

    def after(value, token):
        return lax.optimization_barrier((value, token))[0]

    v_rows = v_factor.reshape(ranks, leaf)
    u_rows = u_factor.reshape(ranks, leaf)

    def h_width(level):
        return ceil_to(rank_k * (levels - 1 - level), LANES)

    groups = leaf // LANES
    s_high, s_low, s_low8, up, down, cores, v_split, a_left = pl.pallas_call(
        functools.partial(interpolation_matrix, levels=levels, rank_k=rank_k),
        in_specs=[scalars()] * 2 + [anywhere()] * 7,
        out_specs=[whole()] * 8,
        out_shape=[
            shape((leaf, width), BF16),
            shape((leaf, width), BF16),
            shape((leaf, width), F8),
            shape((HALO, rhs), BF16),
            shape((HALO, rhs), BF16),
            shape((levels, 2 * rank_k, 2 * rank_k), F32),
            shape((2 * ranks, leaf), BF16),
            shape((leaf, half_rows), BF16),
        ],
        scratch_shapes=[
            pltpu.VMEM((groups, LANES), jnp.int32),
            pltpu.VMEM((3, leaf), jnp.int32),
            pltpu.VMEM((3, leaf), F32),
            pltpu.VMEM((ranks, leaf), F32),
            pltpu.VMEM((groups // 8, LANES, LANES), F32),
            pltpu.VMEM((groups // 8, LANES, LANES), F32),
            pltpu.SemaphoreType.DMA((7 + levels,)),
        ],
        compiler_params=params(8),
        cost_estimate=cost(1e9, 14e6),
        name="interpolation_matrix",
    )(
        device,
        level_rank,
        in_hbm(leaf_order.reshape(groups, LANES)),
        in_hbm(node_index),
        in_hbm(interp_weight),
        in_hbm(modes),
        in_hbm(core_table),
        in_hbm(v_rows),
        in_hbm(leaf_inverse),
    )

    forward = [(i, i + 1) for i in range(count - 1)]
    backward = [(target, source) for source, target in forward]
    rim_low = lax.ppermute(up, "narrow", forward)
    rim_high = lax.ppermute(down, "narrow", backward)

    w, h, left, a_right = pl.pallas_call(
        functools.partial(leaf_operators, levels=levels, rank_k=rank_k),
        in_specs=[scalars(), whole(), anywhere(), whole(), anywhere()],
        out_specs=[whole()] * 4,
        out_shape=[
            shape((2 * ranks, leaf), BF16),
            shape((ranks, h_width(0)), F32),
            shape((leaf, 2 * ranks), BF16),
            shape((leaf, leaf - half_rows), BF16),
        ],
        scratch_shapes=[
            pltpu.VMEM((ranks, leaf), F32),
            pltpu.SemaphoreType.DMA((1 + (leaf - half_rows) // 256,)),
        ],
        compiler_params=params(6),
        cost_estimate=cost(5e9, 14e6),
        name="leaf_operators",
    )(level_rank, v_split, in_hbm(u_rows), a_left, in_hbm(leaf_inverse))

    wide = half + h_width(0)
    mine, send, m, m8 = pl.pallas_call(
        projections,
        in_specs=[scalars()] + [whole()] * 7,
        out_specs=[whole()] * 4,
        out_shape=[
            shape((ranks, wide), F32),
            shape((ranks, wide), F32),
            shape((width, rhs), BF16),
            shape((width, rhs), F8),
        ],
        scratch_shapes=[pltpu.VMEM((2 * ranks, width), BF16), pltpu.VMEM((ranks, rhs), F32)],
        compiler_params=params(8),
        cost_estimate=cost(5e9, 14e6),
        name="projections",
    )(device, w, s_high, s_low, modes, rim_low, rim_high, h)

    def run_interpolate(start, token):
        return pl.pallas_call(
            functools.partial(interpolate, start=start),
            in_specs=[whole()] * 4,
            out_specs=whole(),
            out_shape=shape((half_rows, rhs), BF16),
            compiler_params=params(4),
            cost_estimate=cost(4e9, 8e6),
            name="interpolate",
        )(s_high, s_low8, m, after(m8, token))

    def run_leaf(t0, t1, start, token):
        return pl.pallas_call(
            functools.partial(leaf_solve, start=start),
            in_specs=[whole()] * 4,
            out_specs=whole(),
            out_shape=shape((half_rows, rhs), F32),
            compiler_params=params(4),
            cost_estimate=cost(4.3e9, 10e6),
            name="leaf_solve",
        )(a_left, a_right, t0, after(t1, token))

    def run_stage(level, mine, other, before):
        if level == levels - 1:
            out_shape = [shape((ranks, half), F32)] * 2
            extra = before
        else:
            size = (mine.shape[0] - rank_k, half + h_width(level + 1))
            out_shape = [
                shape(size, F32),
                shape(size, BF16),
                shape((2 if level == 0 else 1, rank_k, half), F32),
            ]
            extra = []
        return pl.pallas_call(
            functools.partial(stage, level=level, levels=levels, rank_k=rank_k, half=half),
            in_specs=[scalars()] + [whole()] * (3 + len(extra)),
            out_specs=[whole()] * len(out_shape),
            out_shape=out_shape,
            compiler_params=params(6),
            cost_estimate=cost(1e8, 1e6),
            name="stage",
        )(device, cores, mine, other, *extra)

    parts = {}

    def beside(position, token):
        if position == 0:
            parts["t0"] = run_interpolate(0, token)
            return parts["t0"]
        if position == 1:
            parts["t1"] = run_interpolate(half_rows, token)
            return parts["t1"]
        if position == 2:
            parts["y0"] = run_leaf(parts["t0"], parts["t1"], 0, token)
            return parts["y0"]
        if position == 3:
            parts["y1"] = run_leaf(parts["t0"], parts["t1"], half_rows, token)
            return parts["y1"]
        return None

    before = []
    for level in range(levels):
        other = partner(send, level)
        token = beside(level, send)
        if token is not None:
            mine = after(mine, token)
        got = run_stage(level, mine, other, before)
        if level < levels - 1:
            mine, send = got[0], got[1]
            before.append(got[2])
    keep, send = got
    crossed = partner(send, 0)

    return pl.pallas_call(
        update,
        in_specs=[scalars()] + [whole()] * 5,
        out_specs=anywhere(),
        out_shape=jax.ShapeDtypeStruct((leaf, rhs), F32),
        scratch_shapes=[
            pltpu.VMEM((3 * ranks, rhs), BF16),
            pltpu.VMEM((leaf, rhs), F32),
            pltpu.SemaphoreType.DMA((leaf // 256,)),
        ],
        compiler_params=params(16),
        cost_estimate=cost(3.3e9, 18e6),
        name="update",
    )(device, left, parts["y0"], parts["y1"], keep, crossed)


def solution(mesh):
    in_specs = (
        P(("groups", "narrow"), None),
        P(None, ("groups", "narrow")),
        P(None, ("groups", "narrow")),
        P(("groups", "narrow")),
        P(("groups", "narrow"), None),
        P(None, None, ("groups", "narrow")),
        P(None, None, ("groups", "narrow")),
        P("groups", None, None),
        P("groups"),
    )
    out_specs = P(("groups", "narrow"), None)
    return jax.shard_map(local, mesh=mesh, in_specs=in_specs, out_specs=out_specs, check_vma=False)
```

profile of v0, /device:TPU:1, one launch (start us, length us, event | category | flops | bytes accessed | tf_op | source)
XLA Modules:
  0.0 72.5 jit_solution(6965643822097965030)
XLA Ops:
  0.0 0.0 copy-start.1
  0.0 0.7 copy-done.1
  0.7 0.0 copy-start.2
  0.7 9.3 %interpolation_matrix.1 = (bf16[2048,1280]{1,0:T(8,128)(2,1)S(1)}, bf16[2048,1280]{1,0:T(8,128)(2,1)S(1)}, f8e4m3fn[2048,1280]{1,0:T(32,128)(4,1)S(1)}, bf16[128...) custom-call(s32[1]{0:T(128)} %bitcast.device_ref, ...), custom_call_target="tpu_custom_call" | custom-call | flops 1000000000 | bytes 14000000 | tf_op jit(solution)/shard_map/interpolation_matrix/pallas_call | solution.py:421
  10.0 4.5 %collective-permute-start = (bf16[128,1024]{1,0:T(8,128)(2,1)S(1)}, bf16[128,1024]{1,0:T(8,128)(2,1)S(1)}, u32[]{:S(2)}, u32[]{:S(2)}) collective-permute-start(bf16[128,1024]{1,0:T(8,128)(2,1)S(1)} %get-tuple-element.48), channel_id=1, source_target_pairs={{0,1},{1,2},{2,3},{3,4},{4,5},{5,6},{6,7},{7,8},{8,9},{9,10},{10,1... | collective-permute-start | bytes 786440 | tf_op jit(solution)/shard_map/ppermute | solution.py:461
  14.5 1.9 %collective-permute-start.1 = (bf16[128,1024]{1,0:T(8,128)(2,1)S(1)}, bf16[128,1024]{1,0:T(8,128)(2,1)S(1)}, u32[]{:S(2)}, u32[]{:S(2)}) collective-permute-start(bf16[128,1024]{1,0:T(8,128)(2,1)S(1)} %get-tuple-element.49), channel_id=1, source_target_pairs={{1,0},{2,1},{3,2},{4,3},{5,4},{6,5},{7,6},{8,7},{9,8},{10,9},{11,1... | collective-permute-start | bytes 786440 | tf_op jit(solution)/shard_map/ppermute | solution.py:462
  16.4 0.0 copy-done.2
  16.4 0.0 copy-start
  16.5 12.1 %leaf_operators.1 = (bf16[512,2048]{1,0:T(8,128)(2,1)S(1)}, f32[256,256]{1,0:T(8,128)S(1)}, bf16[2048,512]{1,0:T(8,128)(2,1)S(1)}, bf16[2048,1024]{1,0:T(8,128)(2,1)S(1)}) custom-call(s32[4]{0:T(128)S(1)} %copy-done.2, bf16[512,2048]{1,0:T(8,128)(2,1)S(1)} %get-tuple-element.40.v_split, f32[256,2048]{1,0:T(8,128)} %bitcast.6, ...), custom_call_target="tpu_custom_call" | custom-call | flops 5000000000 | bytes 14000000 | tf_op jit(solution)/shard_map/leaf_operators/pallas_call | solution.py:464
  28.6 0.0 collective-permute-done.low_ref
  28.6 0.0 collective-permute-done.1.high_ref
  28.6 0.0 copy-done
  28.6 5.7 %projections.1 = (f32[256,768]{1,0:T(8,128)S(1)}, f32[256,768]{1,0:T(8,128)S(1)}, bf16[1280,1024]{1,0:T(8,128)(2,1)S(1)}, f8e4m3fn[1280,1024]{1,0:T(32,128)(4,1)S(1)}) custom-call(s32[1]{0:T(128)} %bitcast.device_ref, bf16[512,2048]{1,0:T(8,128)(2,1)S(1)} %get-tuple-element.46.w_ref, bf16[2048,1280]{1,0:T(8,128)(2,1)S(1)} %get-tuple-element.44.sh_ref, ...), custom_call_target="tpu_custom_call" | custom-call | flops 5000000000 | bytes 14000000 | tf_op jit(solution)/shard_map/projections/pallas_call | solution.py:484
  34.3 0.1 collective-permute-start.2
  34.4 4.5 %interpolate.2.t0_ref = bf16[1024,1024]{1,0:T(8,128)(2,1)S(1)} custom-call(bf16[2048,1280]{1,0:T(8,128)(2,1)S(1)} %get-tuple-element.44.sh_ref, f8e4m3fn[2048,1280]{1,0:T(32,128)(4,1)S(1)} %get-tuple-element.45.s8_ref, bf16[1280,1024]{1,0:T(8,128)(2,1)S(1)} %get-tuple-element.51.m_ref, f8e4m3fn[1280,1024]{1,0:T(32,128)(4,1)S(1)} %get-tuple-element.59.m8_ref), custom_call_target="tpu_custom_call" | custom-call | flops 4000000000 | bytes 8000000 | tf_op jit(solution)/shard_map/interpolate/pallas_call | solution.py:501
  38.9 0.0 collective-permute-done.2.other_ref
  38.9 1.2 %stage.4 = (f32[192,640]{1,0:T(8,128)S(1)}, bf16[192,640]{1,0:T(8,128)(2,1)S(1)}, f32[2,64,512]{2,1,0:T(8,128)S(1)}) custom-call(s32[1]{0:T(128)} %bitcast.device_ref, f32[4,128,128]{2,1,0:T(8,128)S(1)} %get-tuple-element.55.core_ref, f32[256,768]{1,0:T(8,128)S(1)} %get-tuple-element.57.mine_ref, f32[256,768]{1,0:T(8,128)S(1)} %collective-permute-done.2.other_ref), custom_call_target="tpu_custom_call" | custom-call | flops 100000000 | bytes 1000000 | tf_op jit(solution)/shard_map/stage/pallas_call | solution.py:534
  40.0 1.9 %collective-permute-start.3 = (bf16[192,640]{1,0:T(8,128)(2,1)S(1)}, bf16[192,640]{1,0:T(8,128)(2,1)S(1)}, u32[]{:S(2)}, u32[]{:S(2)}) collective-permute-start(bf16[192,640]{1,0:T(8,128)(2,1)S(1)} %get-tuple-element.58), channel_id=1, source_target_pairs={{0,2},{1,3},{2,0},{3,1},{4,6},{5,7},{6,4},{7,5},{8,10},{9,11},{10,... | collective-permute-start | bytes 737288 | tf_op jit(solution)/shard_map/ppermute | solution.py:409
  42.0 4.3 %interpolate.3.t1_ref = bf16[1024,1024]{1,0:T(8,128)(2,1)S(1)} custom-call(bf16[2048,1280]{1,0:T(8,128)(2,1)S(1)} %get-tuple-element.44.sh_ref, f8e4m3fn[2048,1280]{1,0:T(32,128)(4,1)S(1)} %get-tuple-element.45.s8_ref, bf16[1280,1024]{1,0:T(8,128)(2,1)S(1)} %get-tuple-element.51.m_ref, f8e4m3fn[1280,1024]{1,0:T(32,128)(4,1)S(1)} %get-tuple-element.59.m8_ref), custom_call_target="tpu_custom_call" | custom-call | flops 4000000000 | bytes 8000000 | tf_op jit(solution)/shard_map/interpolate/pallas_call | solution.py:501
  46.3 1.7 %collective-permute-done.3.other_ref = bf16[192,640]{1,0:T(8,128)(2,1)S(1)} collective-permute-done((bf16[192,640]{1,0:T(8,128)(2,1)S(1)}, bf16[192,640]{1,0:T(8,128)(2,1)S(1)}, u32[]{:S(2)}, u32[]{:S(2)}) %collective-permute-start.3) | collective-permute-done | bytes 245792 | tf_op jit(solution)/shard_map/ppermute | solution.py:409
  48.0 1.0 %stage.5 = (f32[128,640]{1,0:T(8,128)S(1)}, bf16[128,640]{1,0:T(8,128)(2,1)S(1)}, f32[1,64,512]{2,1,0:T(8,128)S(1)}) custom-call(s32[1]{0:T(128)} %bitcast.device_ref, f32[4,128,128]{2,1,0:T(8,128)S(1)} %get-tuple-element.55.core_ref, f32[192,640]{1,0:T(8,128)S(1)} %get-tuple-element.61.mine_ref, bf16[192,640]{1,0:T(8,128)(2,1)S(1)} %collective-permute-done.3.other_ref), custom_call_target="tpu_custom_call" | custom-call | flops 100000000 | bytes 1000000 | tf_op jit(solution)/shard_map/stage/pallas_call | solution.py:534
  48.9 2.6 %collective-permute-start.4 = (bf16[128,640]{1,0:T(8,128)(2,1)S(1)}, bf16[128,640]{1,0:T(8,128)(2,1)S(1)}, u32[]{:S(2)}, u32[]{:S(2)}) collective-permute-start(bf16[128,640]{1,0:T(8,128)(2,1)S(1)} %get-tuple-element.62), channel_id=1, source_target_pairs={{0,4},{1,5},{2,6},{3,7},{4,0},{5,1},{6,2},{7,3},{8,12},{9,13},{10,... | collective-permute-start | bytes 491528 | tf_op jit(solution)/shard_map/ppermute | solution.py:409
  51.5 4.5 %leaf_solve.2.y0_ref = f32[1024,1024]{1,0:T(8,128)S(1)} custom-call(bf16[2048,1024]{1,0:T(8,128)(2,1)S(1)} %get-tuple-element.41.a0_ref, bf16[2048,1024]{1,0:T(8,128)(2,1)S(1)} %get-tuple-element.43.a1_ref, bf16[1024,1024]{1,0:T(8,128)(2,1)S(1)} %interpolate.2.t0_ref, bf16[1024,1024]{1,0:T(8,128)(2,1)S(1)} %interpolate.3.t1_ref), custom_call_target="tpu_custom_call" | custom-call | flops 4300000256 | bytes 10000000 | tf_op jit(solution)/shard_map/leaf_solve/pallas_call | solution.py:512
  56.0 0.0 collective-permute-done.4.other_ref
  56.1 0.8 %stage.6 = (f32[64,512]{1,0:T(8,128)S(1)}, bf16[64,512]{1,0:T(8,128)(2,1)S(1)}, f32[1,64,512]{2,1,0:T(8,128)S(1)}) custom-call(s32[1]{0:T(128)} %bitcast.device_ref, f32[4,128,128]{2,1,0:T(8,128)S(1)} %get-tuple-element.55.core_ref, f32[128,640]{1,0:T(8,128)S(1)} %get-tuple-element.65.mine_ref, bf16[128,640]{1,0:T(8,128)(2,1)S(1)} %collective-permute-done.4.other_ref), custom_call_target="tpu_custom_call" | custom-call | flops 100000000 | bytes 1000000 | tf_op jit(solution)/shard_map/stage/pallas_call | solution.py:534
  56.8 2.4 %collective-permute-start.5 = (bf16[64,512]{1,0:T(8,128)(2,1)S(1)}, bf16[64,512]{1,0:T(8,128)(2,1)S(1)}, u32[]{:S(2)}, u32[]{:S(2)}) collective-permute-start(bf16[64,512]{1,0:T(8,128)(2,1)S(1)} %get-tuple-element.66), channel_id=1, source_target_pairs={{0,8},{1,9},{2,10},{3,11},{4,12},{5,13},{6,14},{7,15},{8,0},{9,1},... | collective-permute-start | bytes 196616 | tf_op jit(solution)/shard_map/ppermute | solution.py:409
  59.2 4.5 %leaf_solve.3.y1_ref = f32[1024,1024]{1,0:T(8,128)S(1)} custom-call(bf16[2048,1024]{1,0:T(8,128)(2,1)S(1)} %get-tuple-element.41.a0_ref, bf16[2048,1024]{1,0:T(8,128)(2,1)S(1)} %get-tuple-element.43.a1_ref, bf16[1024,1024]{1,0:T(8,128)(2,1)S(1)} %interpolate.2.t0_ref, bf16[1024,1024]{1,0:T(8,128)(2,1)S(1)} %interpolate.3.t1_ref), custom_call_target="tpu_custom_call" | custom-call | flops 4300000256 | bytes 10000000 | tf_op jit(solution)/shard_map/leaf_solve/pallas_call | solution.py:512
  63.7 0.0 collective-permute-done.5.other_ref
  63.7 0.4 stage.7
  64.1 1.4 %collective-permute-start.6 = (f32[256,512]{1,0:T(8,128)S(1)}, f32[256,512]{1,0:T(8,128)S(1)}, u32[]{:S(2)}, u32[]{:S(2)}) collective-permute-start(f32[256,512]{1,0:T(8,128)S(1)} %get-tuple-element.74), channel_id=1, source_target_pairs={{0,1},{1,0},{2,3},{3,2},{4,5},{5,4},{6,7},{7,6},{8,9},{9,8},{10,11... | collective-permute-start | bytes 1572872 | tf_op jit(solution)/shard_map/ppermute | solution.py:409
  65.6 1.5 %collective-permute-done.6.got_ref = f32[256,512]{1,0:T(8,128)S(1)} collective-permute-done((f32[256,512]{1,0:T(8,128)S(1)}, f32[256,512]{1,0:T(8,128)S(1)}, u32[]{:S(2)}, u32[]{:S(2)}) %collective-permute-start.6) | collective-permute-done | bytes 524320 | tf_op jit(solution)/shard_map/ppermute | solution.py:409
  67.1 5.2 %update.1 = f32[2048,1024]{1,0:T(8,128)} custom-call(s32[1]{0:T(128)} %bitcast.device_ref, bf16[2048,512]{1,0:T(8,128)(2,1)S(1)} %get-tuple-element.42.left_ref, f32[1024,1024]{1,0:T(8,128)S(1)} %leaf_solve.2.y0_ref, f32[1024,1024]{1,0:T(8,128)S(1)} %leaf_solve.3.y1_ref, f32[256,512]{1,0:T(8,128)S(1)} %get-tuple-element.73.keep_ref, ...), custom_call_target="tpu_custom_call" | custom-call | flops 3300000000 | bytes 18000000 | tf_op jit(solution)/shard_map/update/pallas_call | solution.py:574
Async XLA Ops:
  0.0 0.7 copy-start.1
  0.7 15.8 %copy-start.2 = (s32[4]{0:T(128)S(1)}, s32[4]{0:T(128)}, u32[]{:S(2)}) copy-start(s32[4]{0:T(128)} %rank_ref.3) | copy-start | bytes 52
  10.0 18.6 %collective-permute-start = (bf16[128,1024]{1,0:T(8,128)(2,1)S(1)}, bf16[128,1024]{1,0:T(8,128)(2,1)S(1)}, u32[]{:S(2)}, u32[]{:S(2)}) collective-permute-start(bf16[128,1024]{1,0:T(8,128)(2,1)S(1)} %get-tuple-element.48), channel_id=1, source_target_pairs={{0,1},{1,2},{2,3},{3,4},{4,5},{5,6},{6,7},{7,8},{8,9},{9,10},{10,1... | collective-permute-start | bytes 786440 | tf_op jit(solution)/shard_map/ppermute | solution.py:461
  14.5 14.1 %collective-permute-start.1 = (bf16[128,1024]{1,0:T(8,128)(2,1)S(1)}, bf16[128,1024]{1,0:T(8,128)(2,1)S(1)}, u32[]{:S(2)}, u32[]{:S(2)}) collective-permute-start(bf16[128,1024]{1,0:T(8,128)(2,1)S(1)} %get-tuple-element.49), channel_id=1, source_target_pairs={{1,0},{2,1},{3,2},{4,3},{5,4},{6,5},{7,6},{8,7},{9,8},{10,9},{11,1... | collective-permute-start | bytes 786440 | tf_op jit(solution)/shard_map/ppermute | solution.py:462
  16.4 12.1 %copy-start = (bf16[1024,1024]{1,0:T(8,128)(2,1)S(1)}, bf16[1024,1024]{1,0:T(8,128)(2,1)}, u32[]{:S(2)}) copy-start(bf16[1024,1024]{1,0:T(8,128)(2,1)} %modes_ref.3) | copy-start | bytes 6291460
  34.3 4.6 %collective-permute-start.2 = (f32[256,768]{1,0:T(8,128)S(1)}, f32[256,768]{1,0:T(8,128)S(1)}, u32[]{:S(2)}, u32[]{:S(2)}) collective-permute-start(f32[256,768]{1,0:T(8,128)S(1)} %get-tuple-element.53), channel_id=1, source_target_pairs={{0,1},{1,0},{2,3},{3,2},{4,5},{5,4},{6,7},{7,6},{8,9},{9,8},{10,11... | collective-permute-start | bytes 2359304 | tf_op jit(solution)/shard_map/ppermute | solution.py:409
  40.0 7.9 %collective-permute-start.3 = (bf16[192,640]{1,0:T(8,128)(2,1)S(1)}, bf16[192,640]{1,0:T(8,128)(2,1)S(1)}, u32[]{:S(2)}, u32[]{:S(2)}) collective-permute-start(bf16[192,640]{1,0:T(8,128)(2,1)S(1)} %get-tuple-element.58), channel_id=1, source_target_pairs={{0,2},{1,3},{2,0},{3,1},{4,6},{5,7},{6,4},{7,5},{8,10},{9,11},{10,... | collective-permute-start | bytes 737288 | tf_op jit(solution)/shard_map/ppermute | solution.py:409
  48.9 7.1 %collective-permute-start.4 = (bf16[128,640]{1,0:T(8,128)(2,1)S(1)}, bf16[128,640]{1,0:T(8,128)(2,1)S(1)}, u32[]{:S(2)}, u32[]{:S(2)}) collective-permute-start(bf16[128,640]{1,0:T(8,128)(2,1)S(1)} %get-tuple-element.62), channel_id=1, source_target_pairs={{0,4},{1,5},{2,6},{3,7},{4,0},{5,1},{6,2},{7,3},{8,12},{9,13},{10,... | collective-permute-start | bytes 491528 | tf_op jit(solution)/shard_map/ppermute | solution.py:409
  56.8 6.9 %collective-permute-start.5 = (bf16[64,512]{1,0:T(8,128)(2,1)S(1)}, bf16[64,512]{1,0:T(8,128)(2,1)S(1)}, u32[]{:S(2)}, u32[]{:S(2)}) collective-permute-start(bf16[64,512]{1,0:T(8,128)(2,1)S(1)} %get-tuple-element.66), channel_id=1, source_target_pairs={{0,8},{1,9},{2,10},{3,11},{4,12},{5,13},{6,14},{7,15},{8,0},{9,1},... | collective-permute-start | bytes 196616 | tf_op jit(solution)/shard_map/ppermute | solution.py:409
  64.1 2.9 %collective-permute-start.6 = (f32[256,512]{1,0:T(8,128)S(1)}, f32[256,512]{1,0:T(8,128)S(1)}, u32[]{:S(2)}, u32[]{:S(2)}) collective-permute-start(f32[256,512]{1,0:T(8,128)S(1)} %get-tuple-element.74), channel_id=1, source_target_pairs={{0,1},{1,0},{2,3},{3,2},{4,5},{5,4},{6,7},{7,6},{8,9},{9,8},{10,11... | collective-permute-start | bytes 1572872 | tf_op jit(solution)/shard_map/ppermute | solution.py:409
where the time goes:
time: 73 us; the launch traced here: 72.5 us
  Pallas kernels  53.5 us (73%)
  starting transfers between devices  14.8 us (20%)
  waiting for transfers between devices  3.21 us (4%)
    pallas_call x1, Pallas kernels, local(): pl.pallas_call(functools.partial(leaf_operators, levels=levels, rank_k=ra...  12.1 us
    pallas_call x1, Pallas kernels, local(): pl.pallas_call(functools.partial(interpolation_matrix, levels=levels, ran...  9.29 us
    pallas_call x2, Pallas kernels, run_leaf(): pl.pallas_call(functools.partial(leaf_solve, start=start), in_specs=[whol...  9.05 us
    pallas_call x2, Pallas kernels, run_interpolate(): pl.pallas_call(functools.partial(interpolate, start=start), in_specs=[who...  8.81 us
    ppermute x5, starting transfers between devices, partner(): lax.ppermute(value, 'narrow', [(s, s ^ 1 << bit) for s in range(count)])  8.35 us
    pallas_call x1, Pallas kernels, local(): pl.pallas_call(projections, in_specs=[scalars()] + [whole()] * 7, out_spe...  5.69 us
    pallas_call x1, Pallas kernels, local(): pl.pallas_call(update, in_specs=[scalars()] + [whole()] * 5, out_specs=an...  5.21 us
    ppermute x1, starting transfers between devices, local(): rim_low = lax.ppermute(up, 'narrow', forward)  4.54 us
  transfers between devices with their start and end apart: 7, of which 2 were waited for; matrix products, arithmetic and copies ran while one was open for 0% of the time, Pallas kernels for 41%

commit v1 on v0

--- a/solution.py
+++ b/solution.py
@@ -13,6 +13,8 @@
 BF16 = jnp.bfloat16
 F8 = jnp.float8_e4m3fn
 LOW_SCALE = 4096.0
+NOWHERE_BITS = 11
+NOWHERE = 2**NOWHERE_BITS - 1
 HIGHEST = lax.Precision.HIGHEST
 MIB = 2**20
 
@@ -77,8 +79,8 @@
     sh_ref,
     sl_ref,
     s8_ref,
-    up_ref,
-    down_ref,
+    inner_ref,
+    outer_ref,
     cores_ref,
     vs_ref,
     a_ref,
@@ -97,6 +99,9 @@
     groups = order_ref.shape[0]
     width = sh_ref.shape[1]
     device = device_ref[0]
+    odd = jnp.bitwise_and(device, 1)
+    inner = pl.multiple_of((1 - odd) * (own - HALO), HALO)
+    outer = pl.multiple_of(odd * (own - HALO), HALO)
     small = [
         pltpu.make_async_copy(order_hbm, order_ref, sems.at[2 + levels]),
         pltpu.make_async_copy(index_hbm, index_ref, sems.at[3 + levels]),
@@ -106,8 +111,8 @@
     cut = a_ref.shape[1]
     a_copy = pltpu.make_async_copy(a_hbm.at[:, pl.ds(0, cut)], a_ref, sems.at[6 + levels])
     copies = [
-        pltpu.make_async_copy(modes_ref.at[pl.ds(own - HALO, HALO)], up_ref, sems.at[0]),
-        pltpu.make_async_copy(modes_ref.at[pl.ds(0, HALO)], down_ref, sems.at[1]),
+        pltpu.make_async_copy(modes_ref.at[pl.ds(inner, HALO)], inner_ref, sems.at[0]),
+        pltpu.make_async_copy(modes_ref.at[pl.ds(outer, HALO)], outer_ref, sems.at[1]),
     ]
     for level in range(levels):
         slot = 2 ** (levels - 1 - level) - 1 + lax.shift_right_logical(device, level + 1)
@@ -143,51 +148,48 @@
                 )
             )
         w = taken[3:]
-        same = cols[2] == cols[0]
-        w[0] = w[0] + jnp.where(same, w[2], 0.0)
-        cols[2] = jnp.where(same, -1, cols[2])
-        same = cols[2] == cols[1]
-        w[1] = w[1] + jnp.where(same, w[2], 0.0)
-        cols[2] = jnp.where(same, -1, cols[2])
-        same = cols[1] == cols[0]
-        w[0] = w[0] + jnp.where(same, w[1], 0.0)
-        cols[1] = jnp.where(same, -1, cols[1])
-        highs = [x.astype(BF16).astype(F32) for x in w]
-        lows = [(x - high) * LOW_SCALE for x, high in zip(w, highs)]
-        for quantity, value in enumerate([x.astype(F32) for x in cols] + highs + lows):
+        for keep, drop in ((0, 2), (1, 2), (0, 1)):
+            same = cols[drop] == cols[keep]
+            w[keep] = w[keep] + jnp.where(same, w[drop], 0.0)
+            cols[drop] = jnp.where(same, NOWHERE, cols[drop])
+        packed = [cols[0] + cols[1] * (NOWHERE + 1), cols[2]]
+        for quantity, value in enumerate([x.astype(F32) for x in packed] + w):
             for r in range(8):
-                at = r * 16 + quantity
-                rows_scr[first // 8, at : at + 1, :] = value[r : r + 1, :]
-    for part in range(groups // 8):
-        cols_scr[part] = rows_scr[part].T
-
-    lane = lax.broadcasted_iota(jnp.int32, (LANES, LANES), 1).astype(jnp.int16)
+                at = (first + r) * 8 + quantity
+                rows_scr[at : at + 1, :] = value[r : r + 1, :]
+    cols_scr[...] = rows_scr[...].T
+
+    lane = lax.broadcasted_iota(jnp.int32, (LANES, LANES), 1)
     zero = jnp.zeros((LANES, LANES), BF16)
-
-    def build(group, carry):
-        part = lax.div(group, 8)
-        turn = lax.rem(LANES - (group - part * 8) * 16, LANES)
-        columns = pltpu.roll(cols_scr[part], turn, axis=1)
+    for group in range(groups):
 
         def spread(j):
-            return jnp.broadcast_to(columns[:, j : j + 1], (LANES, LANES))
-
-        index = [spread(j).astype(jnp.int32).astype(jnp.int16) for j in range(3)]
-        high = [spread(3 + j).astype(BF16) for j in range(3)]
-        low = [spread(6 + j).astype(BF16) for j in range(3)]
-        rows = pl.ds(pl.multiple_of(group * LANES, LANES), LANES)
+            at = group * 8 + j
+            return jnp.broadcast_to(cols_scr[:, at : at + 1], (LANES, LANES))
+
+        both = spread(0).astype(jnp.int32)
+        index = [
+            jnp.bitwise_and(both, NOWHERE),
+            lax.shift_right_logical(both, NOWHERE_BITS),
+            spread(1).astype(jnp.int32),
+        ]
+        index = [i.astype(jnp.int16) for i in index]
+        high, low = [], []
+        for j in range(3):
+            weight = spread(2 + j)
+            high.append(weight.astype(BF16))
+            low.append(((weight - high[j].astype(F32)) * LOW_SCALE).astype(BF16))
+        rows = slice(group * LANES, (group + 1) * LANES)
         for first in range(0, width, LANES):
+            place = (lane + first).astype(jnp.int16)
             s_high, s_low = zero, zero
             for j in range(3):
-                here = (index[j] - jnp.int16(first)) == lane
+                here = index[j] == place
                 s_high = jnp.where(here, high[j], s_high)
                 s_low = jnp.where(here, low[j], s_low)
             sh_ref[rows, first : first + LANES] = s_high
             sl_ref[rows, first : first + LANES] = s_low
             s8_ref[rows, first : first + LANES] = s_low.astype(F8)
-        return carry
-
-    lax.fori_loop(0, groups, build, 0)
     v_copy.wait()
     ranks = levels * rank_k
     for level in range(levels):
@@ -204,18 +206,10 @@
     ranks = levels * rank_k
     piece = 256
     cut = a0_ref.shape[1]
-    pieces = range(0, a1_ref.shape[1], piece)
-    copies = [
-        pltpu.make_async_copy(
-            a_hbm.at[:, pl.ds(cut + first, piece)],
-            a1_ref.at[:, pl.ds(first, piece)],
-            sems.at[1 + first // piece],
-        )
-        for first in pieces
-    ]
-    u_copy = pltpu.make_async_copy(u_hbm, u_ref, sems.at[0])
-    for copy in copies + [u_copy]:
-        copy.start()
+    a_copy = pltpu.make_async_copy(a_hbm.at[:, pl.ds(cut, a1_ref.shape[1])], a1_ref, sems.at[0])
+    u_copy = pltpu.make_async_copy(u_hbm, u_ref, sems.at[1])
+    a_copy.start()
+    u_copy.start()
 
     def product(block, at):
         w = dot(v_split[...], block)
@@ -225,18 +219,20 @@
 
     for first in range(0, cut, piece):
         product(a0_ref[:, first : first + piece], first)
-    for copy, first in zip(copies, pieces):
-        copy.wait()
+    a_copy.wait()
+    for first in range(0, a1_ref.shape[1], piece):
         product(a1_ref[:, first : first + piece], cut + first)
     u_copy.wait()
     for level in range(levels):
         rows = slice(level * rank_k, (level + 1) * rank_k)
         u_ref[rows, :] = masked_level(u_ref, rank_ref, level, rank_k)
+    high, low = split(u_ref[...])
+    part = dot_nt(v_split[...], high)
+    part = part[:ranks] + part[ranks:] + dot_nt(v_split[:ranks, :], low)
     for position, level in enumerate(range(levels - 2, -1, -1)):
-        high, low = split(u_ref[level * rank_k : (level + 1) * rank_k, :])
-        part = dot_nt(v_split[...], high)
-        part = part[:ranks] + part[ranks:] + dot_nt(v_split[:ranks, :], low)
-        h_ref[:, position * rank_k : (position + 1) * rank_k] = part
+        h_ref[:, position * rank_k : (position + 1) * rank_k] = part[
+            :, level * rank_k : (level + 1) * rank_k
+        ]
     used = (levels - 1) * rank_k
     if used < h_ref.shape[1]:
         h_ref[:, used:] = jnp.zeros((ranks, h_ref.shape[1] - used), F32)
@@ -253,8 +249,8 @@
     sh_ref,
     sl_ref,
     modes_ref,
-    low_ref,
-    high_ref,
+    inner_ref,
+    outer_ref,
     h_ref,
     keep_ref,
     send_ref,
@@ -267,8 +263,9 @@
     own = modes_ref.shape[0]
     half = modes_ref.shape[1] // 2
     m_ref[:own, :] = modes_ref[...]
-    m_ref[own : own + HALO, :] = low_ref[...]
-    m_ref[own + HALO :, :] = high_ref[...]
+    core = jnp.bitwise_and(device_ref[0], 1)
+    m_ref[pl.ds(pl.multiple_of(own + HALO - core * HALO, HALO), HALO), :] = inner_ref[...]
+    m_ref[pl.ds(pl.multiple_of(own + core * HALO, HALO), HALO), :] = outer_ref[...]
     m8_ref[...] = m_ref[...].astype(F8)
     piece = 256
     for first in range(0, sh_ref.shape[1], piece):
@@ -283,7 +280,6 @@
         cols = slice(first, first + piece)
         part = dot(ws_scr[...], m_ref[:, cols])
         p_scr[:, cols] = part[:ranks] + part[ranks:]
-    core = jnp.bitwise_and(device_ref[0], 1)
     mine = pl.multiple_of(core * half, half)
     other = pl.multiple_of((1 - core) * half, half)
     keep_ref[:, :half] = p_scr[:, pl.ds(mine, half)]
@@ -343,39 +339,45 @@
 
 def leaf_solve(a0_ref, a1_ref, t0_ref, t1_ref, y_ref, *, start):
     block, piece = 512, 256
+    cut, half = t0_ref.shape[0], a0_ref.shape[1]
     for row in range(0, y_ref.shape[0], block):
         rows = slice(start + row, start + row + block)
         for first in range(0, y_ref.shape[1], piece):
             cols = slice(first, first + piece)
-            part = dot(a0_ref[rows, :], t0_ref[:, cols]) + dot(a1_ref[rows, :], t1_ref[:, cols])
+            part = dot(a0_ref[rows, :cut], t0_ref[:, cols])
+            if cut < half:
+                part = part + dot(a0_ref[rows, cut:], t1_ref[: half - cut, cols])
+            part = part + dot(a1_ref[rows, :], t1_ref[half - cut :, cols])
             y_ref[row : row + block, cols] = part
 
 
-def update(device_ref, left_ref, y0_ref, y1_ref, keep_ref, got_ref, out_ref, c_scr, o_scr, sems):
-    ranks, half = keep_ref.shape
+def update(device_ref, left_ref, y0_ref, y1_ref, c_ref, *refs, own_half):
+    out_ref, c_scr, o_scr, sems = refs[-4:]
+    ranks, half = c_ref.shape
     core = jnp.bitwise_and(device_ref[0], 1)
-    mine = pl.multiple_of(core * half, half)
-    other = pl.multiple_of((1 - core) * half, half)
-    for ref, at in ((keep_ref, mine), (got_ref, other)):
-        high, low = split(ref[...])
-        c_scr[:ranks, pl.ds(at, half)] = high
-        c_scr[ranks : 2 * ranks, pl.ds(at, half)] = high
-        c_scr[2 * ranks :, pl.ds(at, half)] = low
+    at = pl.multiple_of((core if own_half else 1 - core) * half, half)
+    high, low = split(c_ref[...])
+    c_scr[:ranks, :] = high
+    c_scr[ranks : 2 * ranks, :] = high
+    c_scr[2 * ranks :, :] = low
     block, piece = 256, 256
     copies = []
     for row in range(0, o_scr.shape[0], block):
         rows = slice(row, row + block)
         if row < y0_ref.shape[0]:
-            ref, at = y0_ref, row
+            ref, begin = y0_ref, row
         else:
-            ref, at = y1_ref, row - y0_ref.shape[0]
-        for first in range(0, 2 * half, piece):
+            ref, begin = y1_ref, row - y0_ref.shape[0]
+        for first in range(0, half, piece):
             cols = slice(first, first + piece)
             part = dot(left_ref[rows, :], c_scr[: 2 * ranks, cols])
             part = part + dot(left_ref[rows, :ranks], c_scr[2 * ranks :, cols])
-            o_scr[rows, cols] = ref[at : at + block, cols] - part
+            solved = ref[begin : begin + block, pl.ds(pl.multiple_of(at + first, piece), piece)]
+            o_scr[rows, cols] = solved - part
         copy = pltpu.make_async_copy(
-            o_scr.at[pl.ds(row, block)], out_ref.at[pl.ds(row, block)], sems.at[row // block]
+            o_scr.at[pl.ds(row, block)],
+            out_ref.at[pl.ds(row, block), pl.ds(at, half)],
+            sems.at[row // block],
         )
         copy.start()
         copies.append(copy)
@@ -418,7 +420,7 @@
         return ceil_to(rank_k * (levels - 1 - level), LANES)
 
     groups = leaf // LANES
-    s_high, s_low, s_low8, up, down, cores, v_split, a_left = pl.pallas_call(
+    s_high, s_low, s_low8, inner, outer, cores, v_split, a_left = pl.pallas_call(
         functools.partial(interpolation_matrix, levels=levels, rank_k=rank_k),
         in_specs=[scalars()] * 2 + [anywhere()] * 7,
         out_specs=[whole()] * 8,
@@ -437,8 +439,8 @@
             pltpu.VMEM((3, leaf), jnp.int32),
             pltpu.VMEM((3, leaf), F32),
             pltpu.VMEM((ranks, leaf), F32),
-            pltpu.VMEM((groups // 8, LANES, LANES), F32),
-            pltpu.VMEM((groups // 8, LANES, LANES), F32),
+            pltpu.VMEM((groups * 8, LANES), F32),
+            pltpu.VMEM((LANES, groups * 8), F32),
             pltpu.SemaphoreType.DMA((7 + levels,)),
         ],
         compiler_params=params(8),
@@ -456,10 +458,9 @@
         in_hbm(leaf_inverse),
     )
 
-    forward = [(i, i + 1) for i in range(count - 1)]
-    backward = [(target, source) for source, target in forward]
-    rim_low = lax.ppermute(up, "narrow", forward)
-    rim_high = lax.ppermute(down, "narrow", backward)
+    rim_inner = partner(inner, 0)
+    swaps = [(i, i + 1) for i in range(1, count - 1, 2)]
+    rim_outer = lax.ppermute(outer, "narrow", swaps + [(j, i) for i, j in swaps])
 
     w, h, left, a_right = pl.pallas_call(
         functools.partial(leaf_operators, levels=levels, rank_k=rank_k),
@@ -473,9 +474,9 @@
         ],
         scratch_shapes=[
             pltpu.VMEM((ranks, leaf), F32),
-            pltpu.SemaphoreType.DMA((1 + (leaf - half_rows) // 256,)),
+            pltpu.SemaphoreType.DMA((2,)),
         ],
-        compiler_params=params(6),
+        compiler_params=params(10),
         cost_estimate=cost(5e9, 14e6),
         name="leaf_operators",
     )(level_rank, v_split, in_hbm(u_rows), a_left, in_hbm(leaf_inverse))
@@ -495,14 +496,16 @@
         compiler_params=params(8),
         cost_estimate=cost(5e9, 14e6),
         name="projections",
-    )(device, w, s_high, s_low, modes, rim_low, rim_high, h)
-
-    def run_interpolate(start, token):
+    )(device, w, s_high, s_low, modes, rim_inner, rim_outer, h)
+
+    first_rows = leaf // 4
+
+    def run_interpolate(start, size, token):
         return pl.pallas_call(
             functools.partial(interpolate, start=start),
             in_specs=[whole()] * 4,
             out_specs=whole(),
-            out_shape=shape((half_rows, rhs), BF16),
+            out_shape=shape((size, rhs), BF16),
             compiler_params=params(4),
             cost_estimate=cost(4e9, 8e6),
             name="interpolate",
@@ -545,10 +548,10 @@
 
     def beside(position, token):
         if position == 0:
-            parts["t0"] = run_interpolate(0, token)
+            parts["t0"] = run_interpolate(0, first_rows, token)
             return parts["t0"]
         if position == 1:
-            parts["t1"] = run_interpolate(half_rows, token)
+            parts["t1"] = run_interpolate(first_rows, leaf - first_rows, token)
             return parts["t1"]
         if position == 2:
             parts["y0"] = run_leaf(parts["t0"], parts["t1"], 0, token)
@@ -571,20 +574,25 @@
     keep, send = got
     crossed = partner(send, 0)
 
-    return pl.pallas_call(
-        update,
-        in_specs=[scalars()] + [whole()] * 5,
-        out_specs=anywhere(),
-        out_shape=jax.ShapeDtypeStruct((leaf, rhs), F32),
-        scratch_shapes=[
-            pltpu.VMEM((3 * ranks, rhs), BF16),
-            pltpu.VMEM((leaf, rhs), F32),
-            pltpu.SemaphoreType.DMA((leaf // 256,)),
-        ],
-        compiler_params=params(16),
-        cost_estimate=cost(3.3e9, 18e6),
-        name="update",
-    )(device, left, parts["y0"], parts["y1"], keep, crossed)
+    def run_update(c, before, own_half):
+        return pl.pallas_call(
+            functools.partial(update, own_half=own_half),
+            in_specs=[scalars()] + [whole()] * 4 + [anywhere()] * len(before),
+            out_specs=anywhere(),
+            out_shape=pltpu.HBM((leaf, rhs), F32),
+            input_output_aliases={5: 0} if before else {},
+            scratch_shapes=[
+                pltpu.VMEM((3 * ranks, half), BF16),
+                pltpu.VMEM((leaf, half), F32),
+                pltpu.SemaphoreType.DMA((leaf // 256,)),
+            ],
+            compiler_params=params(10),
+            cost_estimate=cost(1.7e9, 9e6),
+            name="update",
+        )(device, left, parts["y0"], parts["y1"], c, *before)
+
+    out = run_update(after(keep, send), [], True)
+    return run_update(crossed, [out], False)
 
 
 def solution(mesh):

time: 73 us -> 59 us (0.81)
  Pallas kernels: 53.5 us -> 46.4 us
  starting transfers between devices: 14.8 us -> 11.3 us
  waiting for transfers between devices: 3.21 us -> 0.06 us
    pallas_call x1, Pallas kernels: 12.1 us -> 7.91 us  [local(): pl.pallas_call(functools.partial(leaf_operators, levels=levels, rank_k=ra...]
    pallas_call x1, Pallas kernels: 9.29 us -> 6.06 us  [local(): pl.pallas_call(functools.partial(interpolation_matrix, levels=levels, ran...]
    ppermute x5 -> x6, waiting for transfers between devices: 3.21 us -> 0.06 us  [partner(): lax.ppermute(value, 'narrow', [(s, s ^ 1 << bit) for s in range(count)])]
    ppermute x2 -> x1, starting transfers between devices: 6.46 us -> 4.67 us  [local(): lax.ppermute(outer, 'narrow', swaps + [(j, i) for i, j in swaps])]
    ppermute x5 -> x6, starting transfers between devices: 8.35 us -> 6.66 us  [partner(): lax.ppermute(value, 'narrow', [(s, s ^ 1 << bit) for s in range(count)])]
    pallas_call x1 -> x2, Pallas kernels: 5.21 us -> 5.46 us  [run_update(): pl.pallas_call(functools.partial(update, own_half=own_half), in_specs=[sc...]
  transfers between devices with their start and end apart: 7 -> 7, of which waited for: 2 -> 0; matrix products, arithmetic and copies ran while one was open for 0% -> 0% of each run, Pallas kernels for 41% -> 49%
where the time goes in v1:
time: 59 us; the launch traced here: 58.8 us
  Pallas kernels  46.4 us (79%)
  starting transfers between devices  11.3 us (19%)
  local copies, waits for them, and re-layouts  0.66 us (1%)
    pallas_call x2, Pallas kernels, run_leaf(): pl.pallas_call(functools.partial(leaf_solve, start=start), in_specs=[whol...  9.12 us
    pallas_call x2, Pallas kernels, run_interpolate(): pl.pallas_call(functools.partial(interpolate, start=start), in_specs=[who...  8.86 us
    pallas_call x1, Pallas kernels, local(): pl.pallas_call(functools.partial(leaf_operators, levels=levels, rank_k=ra...  7.91 us
    ppermute x6, starting transfers between devices, partner(): lax.ppermute(value, 'narrow', [(s, s ^ 1 << bit) for s in range(count)])  6.66 us
    pallas_call x1, Pallas kernels, local(): pl.pallas_call(functools.partial(interpolation_matrix, levels=levels, ran...  6.06 us
    pallas_call x1, Pallas kernels, local(): pl.pallas_call(projections, in_specs=[scalars()] + [whole()] * 7, out_spe...  5.7 us
    pallas_call x2, Pallas kernels, run_update(): pl.pallas_call(functools.partial(update, own_half=own_half), in_specs=[sc...  5.46 us
    ppermute x1, starting transfers between devices, local(): lax.ppermute(outer, 'narrow', swaps + [(j, i) for i, j in swaps])  4.67 us
  transfers between devices with their start and end apart: 7, of which 0 were waited for; matrix products, arithmetic and copies ran while one was open for 0% of the time, Pallas kernels for 49%

profile of v1, /device:TPU:1, one launch (start us, length us, event | category | flops | bytes accessed | tf_op | source)
XLA Modules:
  0.0 58.8 jit_solution(5206788831503785628)
XLA Ops:
  0.0 0.0 copy-start.1
  0.0 0.7 %copy-done.1 = s32[4]{0:T(128)S(1)} copy-done((s32[4]{0:T(128)S(1)}, s32[4]{0:T(128)}, u32[]{:S(2)}) %copy-start.1) | copy-done | bytes 40
  0.7 6.1 %interpolation_matrix.1 = (bf16[2048,1280]{1,0:T(8,128)(2,1)S(1)}, bf16[2048,1280]{1,0:T(8,128)(2,1)S(1)}, f8e4m3fn[2048,1280]{1,0:T(32,128)(4,1)S(1)}, bf16[128...) custom-call(s32[1]{0:T(128)} %bitcast.device_ref, ...), custom_call_target="tpu_custom_call" | custom-call | flops 1000000000 | bytes 14000000 | tf_op jit(solution)/shard_map/interpolation_matrix/pallas_call | solution.py:423
  6.7 0.1 collective-permute-start
  6.8 4.7 %collective-permute-start.1 = (bf16[128,1024]{1,0:T(8,128)(2,1)S(1)}, bf16[128,1024]{1,0:T(8,128)(2,1)S(1)}, u32[]{:S(2)}, u32[]{:S(2)}) collective-permute-start(bf16[128,1024]{1,0:T(8,128)(2,1)S(1)} %get-tuple-element.50), channel_id=1, source_target_pairs={{1,2},{3,4},{5,6},{7,8},{9,10},{11,12},{13,14},{2,1},{4,3},{6,5},{... | collective-permute-start | bytes 786440 | tf_op jit(solution)/shard_map/ppermute | solution.py:463
  11.5 0.0 copy-start
  11.5 7.9 %leaf_operators.1 = (bf16[512,2048]{1,0:T(8,128)(2,1)S(1)}, f32[256,256]{1,0:T(8,128)S(1)}, bf16[2048,512]{1,0:T(8,128)(2,1)S(1)}, bf16[2048,1024]{1,0:T(8,128)(2,1)S(1)}) custom-call(s32[4]{0:T(128)S(1)} %copy-done.1, bf16[512,2048]{1,0:T(8,128)(2,1)S(1)} %get-tuple-element.41.v_split, f32[256,2048]{1,0:T(8,128)} %bitcast.6, ...), custom_call_target="tpu_custom_call" | custom-call | flops 5000000000 | bytes 14000000 | tf_op jit(solution)/shard_map/leaf_operators/pallas_call | solution.py:465
  19.5 0.0 collective-permute-done.inner_ref
  19.5 0.0 collective-permute-done.1.outer_ref
  19.5 0.0 copy-done
  19.5 5.7 %projections.1 = (f32[256,768]{1,0:T(8,128)S(1)}, f32[256,768]{1,0:T(8,128)S(1)}, bf16[1280,1024]{1,0:T(8,128)(2,1)S(1)}, f8e4m3fn[1280,1024]{1,0:T(32,128)(4,1)S(1)}) custom-call(s32[1]{0:T(128)} %bitcast.device_ref, bf16[512,2048]{1,0:T(8,128)(2,1)S(1)} %get-tuple-element.47.w_ref, bf16[2048,1280]{1,0:T(8,128)(2,1)S(1)} %get-tuple-element.45.sh_ref, ...), custom_call_target="tpu_custom_call" | custom-call | flops 5000000000 | bytes 14000000 | tf_op jit(solution)/shard_map/projections/pallas_call | solution.py:485
  25.2 0.1 collective-permute-start.2
  25.3 2.2 %interpolate.2.t0_ref = bf16[512,1024]{1,0:T(8,128)(2,1)S(1)} custom-call(bf16[2048,1280]{1,0:T(8,128)(2,1)S(1)} %get-tuple-element.45.sh_ref, f8e4m3fn[2048,1280]{1,0:T(32,128)(4,1)S(1)} %get-tuple-element.46.s8_ref, bf16[1280,1024]{1,0:T(8,128)(2,1)S(1)} %get-tuple-element.52.m_ref, f8e4m3fn[1280,1024]{1,0:T(32,128)(4,1)S(1)} %get-tuple-element.60.m8_ref), custom_call_target="tpu_custom_call" | custom-call | flops 4000000000 | bytes 8000000 | tf_op jit(solution)/shard_map/interpolate/pallas_call | solution.py:504
  27.5 0.0 collective-permute-done.2.other_ref
  27.6 1.2 %stage.4 = (f32[192,640]{1,0:T(8,128)S(1)}, bf16[192,640]{1,0:T(8,128)(2,1)S(1)}, f32[2,64,512]{2,1,0:T(8,128)S(1)}) custom-call(s32[1]{0:T(128)} %bitcast.device_ref, f32[4,128,128]{2,1,0:T(8,128)S(1)} %get-tuple-element.56.core_ref, f32[256,768]{1,0:T(8,128)S(1)} %get-tuple-element.58.mine_ref, f32[256,768]{1,0:T(8,128)S(1)} %collective-permute-done.2.other_ref), custom_call_target="tpu_custom_call" | custom-call | flops 100000000 | bytes 1000000 | tf_op jit(solution)/shard_map/stage/pallas_call | solution.py:537
  28.7 1.3 %collective-permute-start.3 = (bf16[192,640]{1,0:T(8,128)(2,1)S(1)}, bf16[192,640]{1,0:T(8,128)(2,1)S(1)}, u32[]{:S(2)}, u32[]{:S(2)}) collective-permute-start(bf16[192,640]{1,0:T(8,128)(2,1)S(1)} %get-tuple-element.59), channel_id=1, source_target_pairs={{0,2},{1,3},{2,0},{3,1},{4,6},{5,7},{6,4},{7,5},{8,10},{9,11},{10,... | collective-permute-start | bytes 737288 | tf_op jit(solution)/shard_map/ppermute | solution.py:411
  30.0 6.6 %interpolate.3.t1_ref = bf16[1536,1024]{1,0:T(8,128)(2,1)S(1)} custom-call(bf16[2048,1280]{1,0:T(8,128)(2,1)S(1)} %get-tuple-element.45.sh_ref, f8e4m3fn[2048,1280]{1,0:T(32,128)(4,1)S(1)} %get-tuple-element.46.s8_ref, bf16[1280,1024]{1,0:T(8,128)(2,1)S(1)} %get-tuple-element.52.m_ref, f8e4m3fn[1280,1024]{1,0:T(32,128)(4,1)S(1)} %get-tuple-element.60.m8_ref), custom_call_target="tpu_custom_call" | custom-call | flops 4000000000 | bytes 8000000 | tf_op jit(solution)/shard_map/interpolate/pallas_call | solution.py:504
  36.7 0.0 collective-permute-done.3.other_ref
  36.7 1.0 %stage.5 = (f32[128,640]{1,0:T(8,128)S(1)}, bf16[128,640]{1,0:T(8,128)(2,1)S(1)}, f32[1,64,512]{2,1,0:T(8,128)S(1)}) custom-call(s32[1]{0:T(128)} %bitcast.device_ref, f32[4,128,128]{2,1,0:T(8,128)S(1)} %get-tuple-element.56.core_ref, f32[192,640]{1,0:T(8,128)S(1)} %get-tuple-element.62.mine_ref, bf16[192,640]{1,0:T(8,128)(2,1)S(1)} %collective-permute-done.3.other_ref), custom_call_target="tpu_custom_call" | custom-call | flops 100000000 | bytes 1000000 | tf_op jit(solution)/shard_map/stage/pallas_call | solution.py:537
  37.7 1.4 %collective-permute-start.4 = (bf16[128,640]{1,0:T(8,128)(2,1)S(1)}, bf16[128,640]{1,0:T(8,128)(2,1)S(1)}, u32[]{:S(2)}, u32[]{:S(2)}) collective-permute-start(bf16[128,640]{1,0:T(8,128)(2,1)S(1)} %get-tuple-element.63), channel_id=1, source_target_pairs={{0,4},{1,5},{2,6},{3,7},{4,0},{5,1},{6,2},{7,3},{8,12},{9,13},{10,... | collective-permute-start | bytes 491528 | tf_op jit(solution)/shard_map/ppermute | solution.py:411
  39.1 4.6 %leaf_solve.2.y0_ref = f32[1024,1024]{1,0:T(8,128)S(1)} custom-call(bf16[2048,1024]{1,0:T(8,128)(2,1)S(1)} %get-tuple-element.42.a0_ref, bf16[2048,1024]{1,0:T(8,128)(2,1)S(1)} %get-tuple-element.44.a1_ref, bf16[512,1024]{1,0:T(8,128)(2,1)S(1)} %interpolate.2.t0_ref, bf16[1536,1024]{1,0:T(8,128)(2,1)S(1)} %interpolate.3.t1_ref), custom_call_target="tpu_custom_call" | custom-call | flops 4300000256 | bytes 10000000 | tf_op jit(solution)/shard_map/leaf_solve/pallas_call | solution.py:515
  43.7 0.0 collective-permute-done.4.other_ref
  43.7 0.8 %stage.6 = (f32[64,512]{1,0:T(8,128)S(1)}, bf16[64,512]{1,0:T(8,128)(2,1)S(1)}, f32[1,64,512]{2,1,0:T(8,128)S(1)}) custom-call(s32[1]{0:T(128)} %bitcast.device_ref, f32[4,128,128]{2,1,0:T(8,128)S(1)} %get-tuple-element.56.core_ref, f32[128,640]{1,0:T(8,128)S(1)} %get-tuple-element.66.mine_ref, bf16[128,640]{1,0:T(8,128)(2,1)S(1)} %collective-permute-done.4.other_ref), custom_call_target="tpu_custom_call" | custom-call | flops 100000000 | bytes 1000000 | tf_op jit(solution)/shard_map/stage/pallas_call | solution.py:537
  44.4 2.2 %collective-permute-start.5 = (bf16[64,512]{1,0:T(8,128)(2,1)S(1)}, bf16[64,512]{1,0:T(8,128)(2,1)S(1)}, u32[]{:S(2)}, u32[]{:S(2)}) collective-permute-start(bf16[64,512]{1,0:T(8,128)(2,1)S(1)} %get-tuple-element.67), channel_id=1, source_target_pairs={{0,8},{1,9},{2,10},{3,11},{4,12},{5,13},{6,14},{7,15},{8,0},{9,1},... | collective-permute-start | bytes 196616 | tf_op jit(solution)/shard_map/ppermute | solution.py:411
  46.6 4.6 %leaf_solve.3.y1_ref = f32[1024,1024]{1,0:T(8,128)S(1)} custom-call(bf16[2048,1024]{1,0:T(8,128)(2,1)S(1)} %get-tuple-element.42.a0_ref, bf16[2048,1024]{1,0:T(8,128)(2,1)S(1)} %get-tuple-element.44.a1_ref, bf16[512,1024]{1,0:T(8,128)(2,1)S(1)} %interpolate.2.t0_ref, bf16[1536,1024]{1,0:T(8,128)(2,1)S(1)} %interpolate.3.t1_ref), custom_call_target="tpu_custom_call" | custom-call | flops 4300000256 | bytes 10000000 | tf_op jit(solution)/shard_map/leaf_solve/pallas_call | solution.py:515
  51.2 0.0 collective-permute-done.5.other_ref
  51.2 0.4 stage.7
  51.6 1.6 %collective-permute-start.6 = (f32[256,512]{1,0:T(8,128)S(1)}, f32[256,512]{1,0:T(8,128)S(1)}, u32[]{:S(2)}, u32[]{:S(2)}) collective-permute-start(f32[256,512]{1,0:T(8,128)S(1)} %get-tuple-element.74), channel_id=1, source_target_pairs={{0,1},{1,0},{2,3},{3,2},{4,5},{5,4},{6,7},{7,6},{8,9},{9,8},{10,11... | collective-permute-start | bytes 1572872 | tf_op jit(solution)/shard_map/ppermute | solution.py:411
  53.2 2.7 %update.2.refs_0_ = f32[2048,1024]{1,0:T(8,128)} custom-call(s32[1]{0:T(128)} %bitcast.device_ref, bf16[2048,512]{1,0:T(8,128)(2,1)S(1)} %get-tuple-element.43.left_ref, f32[1024,1024]{1,0:T(8,128)S(1)} %leaf_solve.2.y0_ref, f32[1024,1024]{1,0:T(8,128)S(1)} %leaf_solve.3.y1_ref, f32[256,512]{1,0:T(8,128)S(1)} %get-tuple-element.75.c_ref), custom_call_target="tpu_custom_call" | custom-call | flops 1700000000 | bytes 9000000 | tf_op jit(solution)/shard_map/update/pallas_call | solution.py:578
  55.9 0.0 collective-permute-done.6.c_ref
  55.9 2.7 %update.3 = f32[2048,1024]{1,0:T(8,128)} custom-call(s32[1]{0:T(128)} %bitcast.device_ref, bf16[2048,512]{1,0:T(8,128)(2,1)S(1)} %get-tuple-element.43.left_ref, f32[1024,1024]{1,0:T(8,128)S(1)} %leaf_solve.2.y0_ref, f32[1024,1024]{1,0:T(8,128)S(1)} %leaf_solve.3.y1_ref, ...), custom_call_target="tpu_custom_call", output_to_operand_aliasing={{}: (5, {})} | custom-call | flops 1700000000 | bytes 9000000 | tf_op jit(solution)/shard_map/update/pallas_call | solution.py:578
Async XLA Ops:
  0.0 0.7 %copy-start.1 = (s32[4]{0:T(128)S(1)}, s32[4]{0:T(128)}, u32[]{:S(2)}) copy-start(s32[4]{0:T(128)} %rank_ref.3) | copy-start | bytes 52
  6.7 12.7 %collective-permute-start = (bf16[128,1024]{1,0:T(8,128)(2,1)S(1)}, bf16[128,1024]{1,0:T(8,128)(2,1)S(1)}, u32[]{:S(2)}, u32[]{:S(2)}) collective-permute-start(bf16[128,1024]{1,0:T(8,128)(2,1)S(1)} %get-tuple-element.49), channel_id=1, source_target_pairs={{0,1},{1,0},{2,3},{3,2},{4,5},{5,4},{6,7},{7,6},{8,9},{9,8},{10,11... | collective-permute-start | bytes 786440 | tf_op jit(solution)/shard_map/ppermute | solution.py:411
  6.8 12.6 %collective-permute-start.1 = (bf16[128,1024]{1,0:T(8,128)(2,1)S(1)}, bf16[128,1024]{1,0:T(8,128)(2,1)S(1)}, u32[]{:S(2)}, u32[]{:S(2)}) collective-permute-start(bf16[128,1024]{1,0:T(8,128)(2,1)S(1)} %get-tuple-element.50), channel_id=1, source_target_pairs={{1,2},{3,4},{5,6},{7,8},{9,10},{11,12},{13,14},{2,1},{4,3},{6,5},{... | collective-permute-start | bytes 786440 | tf_op jit(solution)/shard_map/ppermute | solution.py:463
  11.5 8.0 %copy-start = (bf16[1024,1024]{1,0:T(8,128)(2,1)S(1)}, bf16[1024,1024]{1,0:T(8,128)(2,1)}, u32[]{:S(2)}) copy-start(bf16[1024,1024]{1,0:T(8,128)(2,1)} %modes_ref.3) | copy-start | bytes 6291460
  25.2 2.4 %collective-permute-start.2 = (f32[256,768]{1,0:T(8,128)S(1)}, f32[256,768]{1,0:T(8,128)S(1)}, u32[]{:S(2)}, u32[]{:S(2)}) collective-permute-start(f32[256,768]{1,0:T(8,128)S(1)} %get-tuple-element.54), channel_id=1, source_target_pairs={{0,1},{1,0},{2,3},{3,2},{4,5},{5,4},{6,7},{7,6},{8,9},{9,8},{10,11... | collective-permute-start | bytes 2359304 | tf_op jit(solution)/shard_map/ppermute | solution.py:411
  28.7 8.0 %collective-permute-start.3 = (bf16[192,640]{1,0:T(8,128)(2,1)S(1)}, bf16[192,640]{1,0:T(8,128)(2,1)S(1)}, u32[]{:S(2)}, u32[]{:S(2)}) collective-permute-start(bf16[192,640]{1,0:T(8,128)(2,1)S(1)} %get-tuple-element.59), channel_id=1, source_target_pairs={{0,2},{1,3},{2,0},{3,1},{4,6},{5,7},{6,4},{7,5},{8,10},{9,11},{10,... | collective-permute-start | bytes 737288 | tf_op jit(solution)/shard_map/ppermute | solution.py:411
  37.7 6.0 %collective-permute-start.4 = (bf16[128,640]{1,0:T(8,128)(2,1)S(1)}, bf16[128,640]{1,0:T(8,128)(2,1)S(1)}, u32[]{:S(2)}, u32[]{:S(2)}) collective-permute-start(bf16[128,640]{1,0:T(8,128)(2,1)S(1)} %get-tuple-element.63), channel_id=1, source_target_pairs={{0,4},{1,5},{2,6},{3,7},{4,0},{5,1},{6,2},{7,3},{8,12},{9,13},{10,... | collective-permute-start | bytes 491528 | tf_op jit(solution)/shard_map/ppermute | solution.py:411
  44.4 6.7 %collective-permute-start.5 = (bf16[64,512]{1,0:T(8,128)(2,1)S(1)}, bf16[64,512]{1,0:T(8,128)(2,1)S(1)}, u32[]{:S(2)}, u32[]{:S(2)}) collective-permute-start(bf16[64,512]{1,0:T(8,128)(2,1)S(1)} %get-tuple-element.67), channel_id=1, source_target_pairs={{0,8},{1,9},{2,10},{3,11},{4,12},{5,13},{6,14},{7,15},{8,0},{9,1},... | collective-permute-start | bytes 196616 | tf_op jit(solution)/shard_map/ppermute | solution.py:411
  51.6 4.3 %collective-permute-start.6 = (f32[256,512]{1,0:T(8,128)S(1)}, f32[256,512]{1,0:T(8,128)S(1)}, u32[]{:S(2)}, u32[]{:S(2)}) collective-permute-start(f32[256,512]{1,0:T(8,128)S(1)} %get-tuple-element.74), channel_id=1, source_target_pairs={{0,1},{1,0},{2,3},{3,2},{4,5},{5,4},{6,7},{7,6},{8,9},{9,8},{10,11... | collective-permute-start | bytes 1572872 | tf_op jit(solution)/shard_map/ppermute | solution.py:411

commit v2 on v1

--- a/solution.py
+++ b/solution.py
@@ -15,7 +15,6 @@
 LOW_SCALE = 4096.0
 NOWHERE_BITS = 11
 NOWHERE = 2**NOWHERE_BITS - 1
-HIGHEST = lax.Precision.HIGHEST
 MIB = 2**20
 
 
@@ -49,6 +48,12 @@
 
 def dot(a, b):
     return jnp.dot(a, b, preferred_element_type=F32)
+
+
+def dot_split(a, b):
+    a_high, a_low = split(a)
+    b_high, b_low = split(b)
+    return dot(a_high, b_high) + (dot(a_high, b_low) + dot(a_low, b_high))
 
 
 def dot_nt(a, b):
@@ -66,9 +71,9 @@
     return jnp.where(place < rank_ref[level], rows, 0.0)
 
 
-def interpolation_matrix(
+def prepare(
     device_ref,
-    rank_ref,
+    rank_hbm,
     order_hbm,
     index_hbm,
     weight_hbm,
@@ -76,20 +81,18 @@
     core_ref,
     v_hbm,
     a_hbm,
-    sh_ref,
-    sl_ref,
-    s8_ref,
     inner_ref,
     outer_ref,
+    cols_ref,
     cores_ref,
     vs_ref,
     a_ref,
+    rank_ref,
     order_ref,
     index_ref,
     weight_ref,
     v_ref,
     rows_scr,
-    cols_scr,
     sems,
     *,
     levels,
@@ -97,31 +100,31 @@
 ):
     own = modes_ref.shape[0]
     groups = order_ref.shape[0]
-    width = sh_ref.shape[1]
     device = device_ref[0]
     odd = jnp.bitwise_and(device, 1)
     inner = pl.multiple_of((1 - odd) * (own - HALO), HALO)
     outer = pl.multiple_of(odd * (own - HALO), HALO)
-    small = [
-        pltpu.make_async_copy(order_hbm, order_ref, sems.at[2 + levels]),
-        pltpu.make_async_copy(index_hbm, index_ref, sems.at[3 + levels]),
-        pltpu.make_async_copy(weight_hbm, weight_ref, sems.at[4 + levels]),
-    ]
-    v_copy = pltpu.make_async_copy(v_hbm, v_ref, sems.at[5 + levels])
     cut = a_ref.shape[1]
-    a_copy = pltpu.make_async_copy(a_hbm.at[:, pl.ds(0, cut)], a_ref, sems.at[6 + levels])
-    copies = [
-        pltpu.make_async_copy(modes_ref.at[pl.ds(inner, HALO)], inner_ref, sems.at[0]),
-        pltpu.make_async_copy(modes_ref.at[pl.ds(outer, HALO)], outer_ref, sems.at[1]),
+    pairs = [
+        (order_hbm, order_ref),
+        (index_hbm, index_ref),
+        (weight_hbm, weight_ref),
+        (rank_hbm, rank_ref),
+        (v_hbm, v_ref),
+        (modes_ref.at[pl.ds(inner, HALO)], inner_ref),
+        (modes_ref.at[pl.ds(outer, HALO)], outer_ref),
+        (a_hbm.at[:, pl.ds(0, cut)], a_ref),
     ]
     for level in range(levels):
         slot = 2 ** (levels - 1 - level) - 1 + lax.shift_right_logical(device, level + 1)
-        copies.append(
-            pltpu.make_async_copy(core_ref.at[slot], cores_ref.at[level], sems.at[2 + level])
-        )
-    for copy in small + copies + [v_copy, a_copy]:
+        pairs.append((core_ref.at[slot], cores_ref.at[level]))
+    copies = [
+        pltpu.make_async_copy(source, target, sems.at[i])
+        for i, (source, target) in enumerate(pairs)
+    ]
+    for copy in copies:
         copy.start()
-    for copy in small:
+    for copy in copies[:3]:
         copy.wait()
 
     rows_scr[...] = jnp.zeros(rows_scr.shape, F32)
@@ -157,15 +160,62 @@
             for r in range(8):
                 at = (first + r) * 8 + quantity
                 rows_scr[at : at + 1, :] = value[r : r + 1, :]
-    cols_scr[...] = rows_scr[...].T
+    cols_ref[...] = rows_scr[...].T
+
+    for copy in copies[3:5]:
+        copy.wait()
+    ranks = levels * rank_k
+    for level in range(levels):
+        high, low = split(masked_level(v_ref, rank_ref, level, rank_k))
+        vs_ref[level * rank_k : (level + 1) * rank_k, :] = high
+        vs_ref[ranks + level * rank_k : ranks + (level + 1) * rank_k, :] = low
+    for copy in copies[5:]:
+        copy.wait()
+
+
+def leaf_operators(
+    rank_hbm,
+    cols_ref,
+    v_split,
+    u_hbm,
+    a0_ref,
+    a_hbm,
+    sh_ref,
+    sl_ref,
+    s8_ref,
+    w_ref,
+    h_ref,
+    left_ref,
+    a1_ref,
+    rank_ref,
+    u_ref,
+    sems,
+    *,
+    levels,
+    rank_k,
+):
+    ranks = levels * rank_k
+    leaf, width = sh_ref.shape
+    piece = 256
+    cut = a0_ref.shape[1]
+    a_copies = {
+        first: pltpu.make_async_copy(
+            a_hbm.at[:, pl.ds(first, cut)], a1_ref.at[:, pl.ds(first - cut, cut)], sems.at[1 + first // cut]
+        )
+        for first in range(cut, leaf, cut)
+    }
+    rank_copy = pltpu.make_async_copy(rank_hbm, rank_ref, sems.at[0])
+    u_copy = pltpu.make_async_copy(u_hbm, u_ref, sems.at[1])
+    for copy in [rank_copy] + list(a_copies.values()) + [u_copy]:
+        copy.start()
 
     lane = lax.broadcasted_iota(jnp.int32, (LANES, LANES), 1)
     zero = jnp.zeros((LANES, LANES), BF16)
-    for group in range(groups):
-
+
+    def build(group):
         def spread(j):
             at = group * 8 + j
-            return jnp.broadcast_to(cols_scr[:, at : at + 1], (LANES, LANES))
+            return jnp.broadcast_to(cols_ref[:, at : at + 1], (LANES, LANES))
 
         both = spread(0).astype(jnp.int32)
         index = [
@@ -190,38 +240,23 @@
             sh_ref[rows, first : first + LANES] = s_high
             sl_ref[rows, first : first + LANES] = s_low
             s8_ref[rows, first : first + LANES] = s_low.astype(F8)
-    v_copy.wait()
-    ranks = levels * rank_k
-    for level in range(levels):
-        high, low = split(masked_level(v_ref, rank_ref, level, rank_k))
-        vs_ref[level * rank_k : (level + 1) * rank_k, :] = high
-        vs_ref[ranks + level * rank_k : ranks + (level + 1) * rank_k, :] = low
-    for copy in copies + [a_copy]:
-        copy.wait()
-
-
-def leaf_operators(
-    rank_ref, v_split, u_hbm, a0_ref, a_hbm, w_ref, h_ref, left_ref, a1_ref, u_ref, sems, *, levels, rank_k
-):
-    ranks = levels * rank_k
-    piece = 256
-    cut = a0_ref.shape[1]
-    a_copy = pltpu.make_async_copy(a_hbm.at[:, pl.ds(cut, a1_ref.shape[1])], a1_ref, sems.at[0])
-    u_copy = pltpu.make_async_copy(u_hbm, u_ref, sems.at[1])
-    a_copy.start()
-    u_copy.start()
-
-    def product(block, at):
-        w = dot(v_split[...], block)
-        high, low = split(w[:ranks] + w[ranks:])
+
+    for at in range(0, leaf, piece):
+        if at < cut:
+            ref, first = a0_ref, at
+        else:
+            ref, first = a1_ref, at - cut
+        if at in a_copies:
+            a_copies[at].wait()
+        block = slice(first, first + piece)
+        w = dot(v_split[:ranks, :], ref[:, block])
+        build(2 * (at // piece))
+        w = w + dot(v_split[ranks:, :], ref[:, block])
+        build(2 * (at // piece) + 1)
+        high, low = split(w)
         w_ref[:ranks, at : at + piece] = high
         w_ref[ranks:, at : at + piece] = low
-
-    for first in range(0, cut, piece):
-        product(a0_ref[:, first : first + piece], first)
-    a_copy.wait()
-    for first in range(0, a1_ref.shape[1], piece):
-        product(a1_ref[:, first : first + piece], cut + first)
+    rank_copy.wait()
     u_copy.wait()
     for level in range(levels):
         rows = slice(level * rank_k, (level + 1) * rank_k)
@@ -294,7 +329,7 @@
     mine = mine_ref[:rank_k, :half]
     other = other_ref[:rank_k, :half].astype(F32)
     stack = jnp.concatenate([jnp.where(upper, other, mine), jnp.where(upper, mine, other)], axis=0)
-    coef = jnp.dot(core_ref[level], stack, precision=HIGHEST, preferred_element_type=F32)
+    coef = dot_split(core_ref[level], stack)
     c_mine = jnp.where(upper, coef[:rank_k], coef[rank_k:])
     c_other = jnp.where(upper, coef[rank_k:], coef[:rank_k])
     if level < levels - 1:
@@ -303,8 +338,7 @@
         h_mine = mine_ref[rank_k:, at : at + rank_k]
         h_other = other_ref[rank_k:, at : at + rank_k].astype(F32)
         q = mine_ref[rank_k:, :half] + other_ref[rank_k:, :half].astype(F32)
-        q = q - jnp.dot(h_mine, c_mine, precision=HIGHEST, preferred_element_type=F32)
-        q = q - jnp.dot(h_other, c_other, precision=HIGHEST, preferred_element_type=F32)
+        q = q - dot_split(h_mine, c_mine) - dot_split(h_other, c_other)
         next_ref[:, :half] = q
         send_ref[:, :half] = q.astype(send_ref.dtype)
         end = next_ref.shape[1]
@@ -339,15 +373,11 @@
 
 def leaf_solve(a0_ref, a1_ref, t0_ref, t1_ref, y_ref, *, start):
     block, piece = 512, 256
-    cut, half = t0_ref.shape[0], a0_ref.shape[1]
     for row in range(0, y_ref.shape[0], block):
         rows = slice(start + row, start + row + block)
         for first in range(0, y_ref.shape[1], piece):
             cols = slice(first, first + piece)
-            part = dot(a0_ref[rows, :cut], t0_ref[:, cols])
-            if cut < half:
-                part = part + dot(a0_ref[rows, cut:], t1_ref[: half - cut, cols])
-            part = part + dot(a1_ref[rows, :], t1_ref[half - cut :, cols])
+            part = dot(a0_ref[rows, :], t0_ref[:, cols]) + dot(a1_ref[rows, :], t1_ref[:, cols])
             y_ref[row : row + block, cols] = part
 
 
@@ -406,6 +436,7 @@
     width = own + 2 * HALO
     shape = pltpu.VMEM
     half_rows = leaf // 2
+    first_rows = leaf // 4
 
     def partner(value, bit):
         return lax.ppermute(value, "narrow", [(s, s ^ (1 << bit)) for s in range(count)])
@@ -420,35 +451,33 @@
         return ceil_to(rank_k * (levels - 1 - level), LANES)
 
     groups = leaf // LANES
-    s_high, s_low, s_low8, inner, outer, cores, v_split, a_left = pl.pallas_call(
-        functools.partial(interpolation_matrix, levels=levels, rank_k=rank_k),
-        in_specs=[scalars()] * 2 + [anywhere()] * 7,
-        out_specs=[whole()] * 8,
+    inner, outer, columns, cores, v_split, a_left = pl.pallas_call(
+        functools.partial(prepare, levels=levels, rank_k=rank_k),
+        in_specs=[scalars()] + [anywhere()] * 8,
+        out_specs=[whole()] * 6,
         out_shape=[
-            shape((leaf, width), BF16),
-            shape((leaf, width), BF16),
-            shape((leaf, width), F8),
             shape((HALO, rhs), BF16),
             shape((HALO, rhs), BF16),
+            shape((LANES, groups * 8), F32),
             shape((levels, 2 * rank_k, 2 * rank_k), F32),
             shape((2 * ranks, leaf), BF16),
-            shape((leaf, half_rows), BF16),
+            shape((leaf, first_rows), BF16),
         ],
         scratch_shapes=[
+            pltpu.SMEM((levels,), jnp.int32),
             pltpu.VMEM((groups, LANES), jnp.int32),
             pltpu.VMEM((3, leaf), jnp.int32),
             pltpu.VMEM((3, leaf), F32),
             pltpu.VMEM((ranks, leaf), F32),
             pltpu.VMEM((groups * 8, LANES), F32),
-            pltpu.VMEM((LANES, groups * 8), F32),
-            pltpu.SemaphoreType.DMA((7 + levels,)),
+            pltpu.SemaphoreType.DMA((8 + levels,)),
         ],
         compiler_params=params(8),
-        cost_estimate=cost(1e9, 14e6),
-        name="interpolation_matrix",
+        cost_estimate=cost(1e9, 8e6),
+        name="prepare",
     )(
         device,
-        level_rank,
+        in_hbm(level_rank),
         in_hbm(leaf_order.reshape(groups, LANES)),
         in_hbm(node_index),
         in_hbm(interp_weight),
@@ -462,24 +491,28 @@
     swaps = [(i, i + 1) for i in range(1, count - 1, 2)]
     rim_outer = lax.ppermute(outer, "narrow", swaps + [(j, i) for i, j in swaps])
 
-    w, h, left, a_right = pl.pallas_call(
+    s_high, s_low, s_low8, w, h, left, a_right = pl.pallas_call(
         functools.partial(leaf_operators, levels=levels, rank_k=rank_k),
-        in_specs=[scalars(), whole(), anywhere(), whole(), anywhere()],
-        out_specs=[whole()] * 4,
+        in_specs=[anywhere(), whole(), whole(), anywhere(), whole(), anywhere()],
+        out_specs=[whole()] * 7,
         out_shape=[
+            shape((leaf, width), BF16),
+            shape((leaf, width), BF16),
+            shape((leaf, width), F8),
             shape((2 * ranks, leaf), BF16),
             shape((ranks, h_width(0)), F32),
             shape((leaf, 2 * ranks), BF16),
-            shape((leaf, leaf - half_rows), BF16),
+            shape((leaf, leaf - first_rows), BF16),
         ],
         scratch_shapes=[
+            pltpu.SMEM((levels,), jnp.int32),
             pltpu.VMEM((ranks, leaf), F32),
-            pltpu.SemaphoreType.DMA((2,)),
+            pltpu.SemaphoreType.DMA((1 + leaf // first_rows,)),
         ],
-        compiler_params=params(10),
+        compiler_params=params(12),
         cost_estimate=cost(5e9, 14e6),
         name="leaf_operators",
-    )(level_rank, v_split, in_hbm(u_rows), a_left, in_hbm(leaf_inverse))
+    )(in_hbm(level_rank), columns, v_split, in_hbm(u_rows), a_left, in_hbm(leaf_inverse))
 
     wide = half + h_width(0)
     mine, send, m, m8 = pl.pallas_call(
@@ -497,8 +530,6 @@
         cost_estimate=cost(5e9, 14e6),
         name="projections",
     )(device, w, s_high, s_low, modes, rim_inner, rim_outer, h)
-
-    first_rows = leaf // 4
 
     def run_interpolate(start, size, token):
         return pl.pallas_call(

time: 59 us -> 54.6 us (0.925)
  Pallas kernels: 46.4 us -> 42.7 us
  local copies, waits for them, and re-layouts: 0.66 us -> 0.01 us
    pallas_call x1, Pallas kernels: 6.06 us -> 2.55 us  [local(): pl.pallas_call(functools.partial(prepare, levels=levels, rank_k=rank_k),...]
    pallas_call x4, Pallas kernels: 3.31 us -> 2.14 us  [run_stage(): pl.pallas_call(functools.partial(stage, level=level, levels=levels, rank_...]
    pallas_call x1, Pallas kernels: 7.91 us -> 9.07 us  [local(): pl.pallas_call(functools.partial(leaf_operators, levels=levels, rank_k=ra...]
    unnamed x4 -> x2, local copies, waits for them, and re-layouts: 0.66 us -> 0.01 us
  transfers between devices with their start and end apart: 7 -> 7, of which waited for: 0 -> 0; matrix products, arithmetic and copies ran while one was open for 0% -> 0% of each run, Pallas kernels for 49% -> 54%
where the time goes in v2:
time: 54.6 us; the launch traced here: 54.4 us
  Pallas kernels  42.7 us (78%)
  starting transfers between devices  11.4 us (21%)
    pallas_call x1, Pallas kernels, local(): pl.pallas_call(functools.partial(leaf_operators, levels=levels, rank_k=ra...  9.07 us
    pallas_call x2, Pallas kernels, run_leaf(): pl.pallas_call(functools.partial(leaf_solve, start=start), in_specs=[whol...  8.97 us
    pallas_call x2, Pallas kernels, run_interpolate(): pl.pallas_call(functools.partial(interpolate, start=start), in_specs=[who...  8.86 us
    ppermute x6, starting transfers between devices, partner(): lax.ppermute(value, 'narrow', [(s, s ^ 1 << bit) for s in range(count)])  6.87 us
    pallas_call x1, Pallas kernels, local(): pl.pallas_call(projections, in_specs=[scalars()] + [whole()] * 7, out_spe...  5.67 us
    pallas_call x2, Pallas kernels, run_update(): pl.pallas_call(functools.partial(update, own_half=own_half), in_specs=[sc...  5.45 us
    ppermute x1, starting transfers between devices, local(): lax.ppermute(outer, 'narrow', swaps + [(j, i) for i, j in swaps])  4.49 us
    pallas_call x1, Pallas kernels, local(): pl.pallas_call(functools.partial(prepare, levels=levels, rank_k=rank_k),...  2.55 us
  transfers between devices with their start and end apart: 7, of which 0 were waited for; matrix products, arithmetic and copies ran while one was open for 0% of the time, Pallas kernels for 54%

profile of v2, /device:TPU:1, one launch (start us, length us, event | category | flops | bytes accessed | tf_op | source)
XLA Modules:
  0.0 54.4 jit_solution(1413213360111651373)
XLA Ops:
  0.0 2.5 %prepare.1 = (bf16[128,1024]{1,0:T(8,128)(2,1)S(1)}, bf16[128,1024]{1,0:T(8,128)(2,1)S(1)}, f32[128,128]{1,0:T(8,128)S(1)}, f32[4,128,128]{2,1,0:T(8,128)S(1)}, ...) custom-call(s32[1]{0:T(128)} %bitcast.device_ref, s32[4]{0:T(128)} %rank_hbm.3, s32[16,128]{1,0:T(8,128)} %bitcast.5, ...), custom_call_target="tpu_custom_call" | custom-call | flops 1000000000 | bytes 8000000 | tf_op jit(solution)/shard_map/prepare/pallas_call | solution.py:454
  2.6 0.1 collective-permute-start
  2.7 4.5 %collective-permute-start.1 = (bf16[128,1024]{1,0:T(8,128)(2,1)S(1)}, bf16[128,1024]{1,0:T(8,128)(2,1)S(1)}, u32[]{:S(2)}, u32[]{:S(2)}) collective-permute-start(bf16[128,1024]{1,0:T(8,128)(2,1)S(1)} %get-tuple-element.52), channel_id=1, source_target_pairs={{1,2},{3,4},{5,6},{7,8},{9,10},{11,12},{13,14},{2,1},{4,3},{6,5},{... | collective-permute-start | bytes 786440 | tf_op jit(solution)/shard_map/ppermute | solution.py:492
  7.2 0.0 copy-start
  7.2 9.1 %leaf_operators.1 = (bf16[2048,1280]{1,0:T(8,128)(2,1)S(1)}, bf16[2048,1280]{1,0:T(8,128)(2,1)S(1)}, f8e4m3fn[2048,1280]{1,0:T(32,128)(4,1)S(1)}, bf16[512,2048]...) custom-call(s32[4]{0:T(128)} %rank_hbm.3, ...), custom_call_target="tpu_custom_call" | custom-call | flops 5000000000 | bytes 14000000 | tf_op jit(solution)/shard_map/leaf_operators/pallas_call | solution.py:494
  16.3 0.0 collective-permute-done.inner_ref
  16.3 0.0 collective-permute-done.1.outer_ref
  16.3 0.0 copy-done
  16.3 5.7 %projections.1 = (f32[256,768]{1,0:T(8,128)S(1)}, f32[256,768]{1,0:T(8,128)S(1)}, bf16[1280,1024]{1,0:T(8,128)(2,1)S(1)}, f8e4m3fn[1280,1024]{1,0:T(32,128)(4,1)S(1)}) custom-call(s32[1]{0:T(128)} %bitcast.device_ref, bf16[512,2048]{1,0:T(8,128)(2,1)S(1)} %get-tuple-element.49.w_ref, bf16[2048,1280]{1,0:T(8,128)(2,1)S(1)} %get-tuple-element.47.sh_ref, ...), custom_call_target="tpu_custom_call" | custom-call | flops 5000000000 | bytes 14000000 | tf_op jit(solution)/shard_map/projections/pallas_call | solution.py:518
  22.0 0.1 collective-permute-start.2
  22.1 2.4 %interpolate.2.t0_ref = bf16[512,1024]{1,0:T(8,128)(2,1)S(1)} custom-call(bf16[2048,1280]{1,0:T(8,128)(2,1)S(1)} %get-tuple-element.47.sh_ref, f8e4m3fn[2048,1280]{1,0:T(32,128)(4,1)S(1)} %get-tuple-element.48.s8_ref, bf16[1280,1024]{1,0:T(8,128)(2,1)S(1)} %get-tuple-element.54.m_ref, f8e4m3fn[1280,1024]{1,0:T(32,128)(4,1)S(1)} %get-tuple-element.62.m8_ref), custom_call_target="tpu_custom_call" | custom-call | flops 4000000000 | bytes 8000000 | tf_op jit(solution)/shard_map/interpolate/pallas_call | solution.py:535
  24.5 0.0 collective-permute-done.2.other_ref
  24.5 0.7 %stage.4 = (f32[192,640]{1,0:T(8,128)S(1)}, bf16[192,640]{1,0:T(8,128)(2,1)S(1)}, f32[2,64,512]{2,1,0:T(8,128)S(1)}) custom-call(s32[1]{0:T(128)} %bitcast.device_ref, f32[4,128,128]{2,1,0:T(8,128)S(1)} %get-tuple-element.58.core_ref, f32[256,768]{1,0:T(8,128)S(1)} %get-tuple-element.60.mine_ref, f32[256,768]{1,0:T(8,128)S(1)} %collective-permute-done.2.other_ref), custom_call_target="tpu_custom_call" | custom-call | flops 100000000 | bytes 1000000 | tf_op jit(solution)/shard_map/stage/pallas_call | solution.py:568
  25.2 1.3 %collective-permute-start.3 = (bf16[192,640]{1,0:T(8,128)(2,1)S(1)}, bf16[192,640]{1,0:T(8,128)(2,1)S(1)}, u32[]{:S(2)}, u32[]{:S(2)}) collective-permute-start(bf16[192,640]{1,0:T(8,128)(2,1)S(1)} %get-tuple-element.61), channel_id=1, source_target_pairs={{0,2},{1,3},{2,0},{3,1},{4,6},{5,7},{6,4},{7,5},{8,10},{9,11},{10,... | collective-permute-start | bytes 737288 | tf_op jit(solution)/shard_map/ppermute | solution.py:442
  26.5 6.5 %interpolate.3.t1_ref = bf16[1536,1024]{1,0:T(8,128)(2,1)S(1)} custom-call(bf16[2048,1280]{1,0:T(8,128)(2,1)S(1)} %get-tuple-element.47.sh_ref, f8e4m3fn[2048,1280]{1,0:T(32,128)(4,1)S(1)} %get-tuple-element.48.s8_ref, bf16[1280,1024]{1,0:T(8,128)(2,1)S(1)} %get-tuple-element.54.m_ref, f8e4m3fn[1280,1024]{1,0:T(32,128)(4,1)S(1)} %get-tuple-element.62.m8_ref), custom_call_target="tpu_custom_call" | custom-call | flops 4000000000 | bytes 8000000 | tf_op jit(solution)/shard_map/interpolate/pallas_call | solution.py:535
  33.0 0.0 collective-permute-done.3.other_ref
  33.0 0.6 %stage.5 = (f32[128,640]{1,0:T(8,128)S(1)}, bf16[128,640]{1,0:T(8,128)(2,1)S(1)}, f32[1,64,512]{2,1,0:T(8,128)S(1)}) custom-call(s32[1]{0:T(128)} %bitcast.device_ref, f32[4,128,128]{2,1,0:T(8,128)S(1)} %get-tuple-element.58.core_ref, f32[192,640]{1,0:T(8,128)S(1)} %get-tuple-element.64.mine_ref, bf16[192,640]{1,0:T(8,128)(2,1)S(1)} %collective-permute-done.3.other_ref), custom_call_target="tpu_custom_call" | custom-call | flops 100000000 | bytes 1000000 | tf_op jit(solution)/shard_map/stage/pallas_call | solution.py:568
  33.6 1.4 %collective-permute-start.4 = (bf16[128,640]{1,0:T(8,128)(2,1)S(1)}, bf16[128,640]{1,0:T(8,128)(2,1)S(1)}, u32[]{:S(2)}, u32[]{:S(2)}) collective-permute-start(bf16[128,640]{1,0:T(8,128)(2,1)S(1)} %get-tuple-element.65), channel_id=1, source_target_pairs={{0,4},{1,5},{2,6},{3,7},{4,0},{5,1},{6,2},{7,3},{8,12},{9,13},{10,... | collective-permute-start | bytes 491528 | tf_op jit(solution)/shard_map/ppermute | solution.py:442
  35.0 4.5 %leaf_solve.2.y0_ref = f32[1024,1024]{1,0:T(8,128)S(1)} custom-call(bf16[2048,512]{1,0:T(8,128)(2,1)S(1)} %get-tuple-element.44.a0_ref, bf16[2048,1536]{1,0:T(8,128)(2,1)S(1)} %get-tuple-element.46.a1_ref, bf16[512,1024]{1,0:T(8,128)(2,1)S(1)} %interpolate.2.t0_ref, bf16[1536,1024]{1,0:T(8,128)(2,1)S(1)} %interpolate.3.t1_ref), custom_call_target="tpu_custom_call" | custom-call | flops 4300000256 | bytes 10000000 | tf_op jit(solution)/shard_map/leaf_solve/pallas_call | solution.py:546
  39.5 0.0 collective-permute-done.4.other_ref
  39.5 0.5 stage.6
  40.1 2.4 %collective-permute-start.5 = (bf16[64,512]{1,0:T(8,128)(2,1)S(1)}, bf16[64,512]{1,0:T(8,128)(2,1)S(1)}, u32[]{:S(2)}, u32[]{:S(2)}) collective-permute-start(bf16[64,512]{1,0:T(8,128)(2,1)S(1)} %get-tuple-element.69), channel_id=1, source_target_pairs={{0,8},{1,9},{2,10},{3,11},{4,12},{5,13},{6,14},{7,15},{8,0},{9,1},... | collective-permute-start | bytes 196616 | tf_op jit(solution)/shard_map/ppermute | solution.py:442
  42.4 4.5 %leaf_solve.3.y1_ref = f32[1024,1024]{1,0:T(8,128)S(1)} custom-call(bf16[2048,512]{1,0:T(8,128)(2,1)S(1)} %get-tuple-element.44.a0_ref, bf16[2048,1536]{1,0:T(8,128)(2,1)S(1)} %get-tuple-element.46.a1_ref, bf16[512,1024]{1,0:T(8,128)(2,1)S(1)} %interpolate.2.t0_ref, bf16[1536,1024]{1,0:T(8,128)(2,1)S(1)} %interpolate.3.t1_ref), custom_call_target="tpu_custom_call" | custom-call | flops 4300000256 | bytes 10000000 | tf_op jit(solution)/shard_map/leaf_solve/pallas_call | solution.py:546
  46.9 0.0 collective-permute-done.5.other_ref
  46.9 0.3 stage.7
  47.2 1.6 %collective-permute-start.6 = (f32[256,512]{1,0:T(8,128)S(1)}, f32[256,512]{1,0:T(8,128)S(1)}, u32[]{:S(2)}, u32[]{:S(2)}) collective-permute-start(f32[256,512]{1,0:T(8,128)S(1)} %get-tuple-element.76), channel_id=1, source_target_pairs={{0,1},{1,0},{2,3},{3,2},{4,5},{5,4},{6,7},{7,6},{8,9},{9,8},{10,11... | collective-permute-start | bytes 1572872 | tf_op jit(solution)/shard_map/ppermute | solution.py:442
  48.8 2.7 %update.2.refs_0_ = f32[2048,1024]{1,0:T(8,128)} custom-call(s32[1]{0:T(128)} %bitcast.device_ref, bf16[2048,512]{1,0:T(8,128)(2,1)S(1)} %get-tuple-element.45.left_ref, f32[1024,1024]{1,0:T(8,128)S(1)} %leaf_solve.2.y0_ref, f32[1024,1024]{1,0:T(8,128)S(1)} %leaf_solve.3.y1_ref, f32[256,512]{1,0:T(8,128)S(1)} %get-tuple-element.77.c_ref), custom_call_target="tpu_custom_call" | custom-call | flops 1700000000 | bytes 9000000 | tf_op jit(solution)/shard_map/update/pallas_call | solution.py:609
  51.5 0.0 collective-permute-done.6.c_ref
  51.5 2.7 %update.3 = f32[2048,1024]{1,0:T(8,128)} custom-call(s32[1]{0:T(128)} %bitcast.device_ref, bf16[2048,512]{1,0:T(8,128)(2,1)S(1)} %get-tuple-element.45.left_ref, f32[1024,1024]{1,0:T(8,128)S(1)} %leaf_solve.2.y0_ref, f32[1024,1024]{1,0:T(8,128)S(1)} %leaf_solve.3.y1_ref, ...), custom_call_target="tpu_custom_call", output_to_operand_aliasing={{}: (5, {})} | custom-call | flops 1700000000 | bytes 9000000 | tf_op jit(solution)/shard_map/update/pallas_call | solution.py:609
Async XLA Ops:
  2.6 13.7 %collective-permute-start = (bf16[128,1024]{1,0:T(8,128)(2,1)S(1)}, bf16[128,1024]{1,0:T(8,128)(2,1)S(1)}, u32[]{:S(2)}, u32[]{:S(2)}) collective-permute-start(bf16[128,1024]{1,0:T(8,128)(2,1)S(1)} %get-tuple-element.51), channel_id=1, source_target_pairs={{0,1},{1,0},{2,3},{3,2},{4,5},{5,4},{6,7},{7,6},{8,9},{9,8},{10,11... | collective-permute-start | bytes 786440 | tf_op jit(solution)/shard_map/ppermute | solution.py:442
  2.7 13.6 %collective-permute-start.1 = (bf16[128,1024]{1,0:T(8,128)(2,1)S(1)}, bf16[128,1024]{1,0:T(8,128)(2,1)S(1)}, u32[]{:S(2)}, u32[]{:S(2)}) collective-permute-start(bf16[128,1024]{1,0:T(8,128)(2,1)S(1)} %get-tuple-element.52), channel_id=1, source_target_pairs={{1,2},{3,4},{5,6},{7,8},{9,10},{11,12},{13,14},{2,1},{4,3},{6,5},{... | collective-permute-start | bytes 786440 | tf_op jit(solution)/shard_map/ppermute | solution.py:492
  7.2 9.1 %copy-start = (bf16[1024,1024]{1,0:T(8,128)(2,1)S(1)}, bf16[1024,1024]{1,0:T(8,128)(2,1)}, u32[]{:S(2)}) copy-start(bf16[1024,1024]{1,0:T(8,128)(2,1)} %modes_ref.3) | copy-start | bytes 6291460
  22.0 2.5 %collective-permute-start.2 = (f32[256,768]{1,0:T(8,128)S(1)}, f32[256,768]{1,0:T(8,128)S(1)}, u32[]{:S(2)}, u32[]{:S(2)}) collective-permute-start(f32[256,768]{1,0:T(8,128)S(1)} %get-tuple-element.56), channel_id=1, source_target_pairs={{0,1},{1,0},{2,3},{3,2},{4,5},{5,4},{6,7},{7,6},{8,9},{9,8},{10,11... | collective-permute-start | bytes 2359304 | tf_op jit(solution)/shard_map/ppermute | solution.py:442
  25.2 7.8 %collective-permute-start.3 = (bf16[192,640]{1,0:T(8,128)(2,1)S(1)}, bf16[192,640]{1,0:T(8,128)(2,1)S(1)}, u32[]{:S(2)}, u32[]{:S(2)}) collective-permute-start(bf16[192,640]{1,0:T(8,128)(2,1)S(1)} %get-tuple-element.61), channel_id=1, source_target_pairs={{0,2},{1,3},{2,0},{3,1},{4,6},{5,7},{6,4},{7,5},{8,10},{9,11},{10,... | collective-permute-start | bytes 737288 | tf_op jit(solution)/shard_map/ppermute | solution.py:442
  33.6 5.9 %collective-permute-start.4 = (bf16[128,640]{1,0:T(8,128)(2,1)S(1)}, bf16[128,640]{1,0:T(8,128)(2,1)S(1)}, u32[]{:S(2)}, u32[]{:S(2)}) collective-permute-start(bf16[128,640]{1,0:T(8,128)(2,1)S(1)} %get-tuple-element.65), channel_id=1, source_target_pairs={{0,4},{1,5},{2,6},{3,7},{4,0},{5,1},{6,2},{7,3},{8,12},{9,13},{10,... | collective-permute-start | bytes 491528 | tf_op jit(solution)/shard_map/ppermute | solution.py:442
  40.1 6.9 %collective-permute-start.5 = (bf16[64,512]{1,0:T(8,128)(2,1)S(1)}, bf16[64,512]{1,0:T(8,128)(2,1)S(1)}, u32[]{:S(2)}, u32[]{:S(2)}) collective-permute-start(bf16[64,512]{1,0:T(8,128)(2,1)S(1)} %get-tuple-element.69), channel_id=1, source_target_pairs={{0,8},{1,9},{2,10},{3,11},{4,12},{5,13},{6,14},{7,15},{8,0},{9,1},... | collective-permute-start | bytes 196616 | tf_op jit(solution)/shard_map/ppermute | solution.py:442
  47.2 4.3 %collective-permute-start.6 = (f32[256,512]{1,0:T(8,128)S(1)}, f32[256,512]{1,0:T(8,128)S(1)}, u32[]{:S(2)}, u32[]{:S(2)}) collective-permute-start(f32[256,512]{1,0:T(8,128)S(1)} %get-tuple-element.76), channel_id=1, source_target_pairs={{0,1},{1,0},{2,3},{3,2},{4,5},{5,4},{6,7},{7,6},{8,9},{9,8},{10,11... | collective-permute-start | bytes 1572872 | tf_op jit(solution)/shard_map/ppermute | solution.py:442

commit v3 on v2

--- a/solution.py
+++ b/solution.py
@@ -13,6 +13,8 @@
 BF16 = jnp.bfloat16
 F8 = jnp.float8_e4m3fn
 LOW_SCALE = 4096.0
+W8_TOP = 224.0
+TINY = 1e-30
 NOWHERE_BITS = 11
 NOWHERE = 2**NOWHERE_BITS - 1
 MIB = 2**20
@@ -181,7 +183,6 @@
     a0_ref,
     a_hbm,
     sh_ref,
-    sl_ref,
     s8_ref,
     w_ref,
     h_ref,
@@ -238,7 +239,6 @@
                 s_high = jnp.where(here, high[j], s_high)
                 s_low = jnp.where(here, low[j], s_low)
             sh_ref[rows, first : first + LANES] = s_high
-            sl_ref[rows, first : first + LANES] = s_low
             s8_ref[rows, first : first + LANES] = s_low.astype(F8)
 
     for at in range(0, leaf, piece):
@@ -282,7 +282,7 @@
     device_ref,
     w_ref,
     sh_ref,
-    sl_ref,
+    s8_ref,
     modes_ref,
     inner_ref,
     outer_ref,
@@ -291,6 +291,7 @@
     send_ref,
     m_ref,
     m8_ref,
+    w8_scr,
     ws_scr,
     p_scr,
 ):
@@ -303,11 +304,22 @@
     m_ref[pl.ds(pl.multiple_of(own + core * HALO, HALO), HALO), :] = outer_ref[...]
     m8_ref[...] = m_ref[...].astype(F8)
     piece = 256
-    for first in range(0, sh_ref.shape[1], piece):
-        cols = slice(first, first + piece)
+    pieces = [slice(first, first + piece) for first in range(0, sh_ref.shape[1], piece)]
+
+    def main_part(cols):
         part = dot(w_ref[...], sh_ref[:, cols])
-        part = part[:ranks] + part[ranks:]
-        part = part + dot(w_ref[:ranks, :], sl_ref[:, cols]) * (1.0 / LOW_SCALE)
+        return part[:ranks] + part[ranks:]
+
+    parts = [main_part(pieces[0])]
+    largest = jnp.max(jnp.abs(w_ref[:ranks, :].astype(F32)), axis=1, keepdims=True)
+    largest = jnp.maximum(largest, TINY)
+    parts.append(main_part(pieces[1]))
+    w8_scr[...] = (w_ref[:ranks, :].astype(F32) * (W8_TOP / largest)).astype(F8)
+    w_back = largest * (1.0 / (W8_TOP * LOW_SCALE))
+    for i, cols in enumerate(pieces):
+        if i + 2 < len(pieces):
+            parts.append(main_part(pieces[i + 2]))
+        part = parts[i] + dot(w8_scr[...], s8_ref[:, cols]) * w_back
         high, low = split(part)
         ws_scr[:ranks, cols] = high
         ws_scr[ranks:, cols] = low
@@ -491,12 +503,11 @@
     swaps = [(i, i + 1) for i in range(1, count - 1, 2)]
     rim_outer = lax.ppermute(outer, "narrow", swaps + [(j, i) for i, j in swaps])
 
-    s_high, s_low, s_low8, w, h, left, a_right = pl.pallas_call(
+    s_high, s_low8, w, h, left, a_right = pl.pallas_call(
         functools.partial(leaf_operators, levels=levels, rank_k=rank_k),
         in_specs=[anywhere(), whole(), whole(), anywhere(), whole(), anywhere()],
-        out_specs=[whole()] * 7,
+        out_specs=[whole()] * 6,
         out_shape=[
-            shape((leaf, width), BF16),
             shape((leaf, width), BF16),
             shape((leaf, width), F8),
             shape((2 * ranks, leaf), BF16),
@@ -525,11 +536,15 @@
             shape((width, rhs), BF16),
             shape((width, rhs), F8),
         ],
-        scratch_shapes=[pltpu.VMEM((2 * ranks, width), BF16), pltpu.VMEM((ranks, rhs), F32)],
+        scratch_shapes=[
+            pltpu.VMEM((ranks, leaf), F8),
+            pltpu.VMEM((2 * ranks, width), BF16),
+            pltpu.VMEM((ranks, rhs), F32),
+        ],
         compiler_params=params(8),
         cost_estimate=cost(5e9, 14e6),
         name="projections",
-    )(device, w, s_high, s_low, modes, rim_inner, rim_outer, h)
+    )(device, w, s_high, s_low8, modes, rim_inner, rim_outer, h)
 
     def run_interpolate(start, size, token):
         return pl.pallas_call(

time: 54.6 us -> 53.9 us (0.987)
  Pallas kernels: 42.7 us -> 42 us
  transfers between devices with their start and end apart: 7 -> 7, of which waited for: 0 -> 0; matrix products, arithmetic and copies ran while one was open for 0% -> 0% of each run, Pallas kernels for 54% -> 55%
where the time goes in v3:
time: 53.9 us; the launch traced here: 53.7 us
  Pallas kernels  42 us (78%)
  starting transfers between devices  11.4 us (21%)
    pallas_call x2, Pallas kernels, run_leaf(): pl.pallas_call(functools.partial(leaf_solve, start=start), in_specs=[whol...  9.12 us
    pallas_call x2, Pallas kernels, run_interpolate(): pl.pallas_call(functools.partial(interpolate, start=start), in_specs=[who...  8.83 us
    pallas_call x1, Pallas kernels, local(): pl.pallas_call(functools.partial(leaf_operators, levels=levels, rank_k=ra...  8.72 us
    ppermute x6, starting transfers between devices, partner(): lax.ppermute(value, 'narrow', [(s, s ^ 1 << bit) for s in range(count)])  6.92 us
    pallas_call x2, Pallas kernels, run_update(): pl.pallas_call(functools.partial(update, own_half=own_half), in_specs=[sc...  5.46 us
    pallas_call x1, Pallas kernels, local(): pl.pallas_call(projections, in_specs=[scalars()] + [whole()] * 7, out_spe...  5.16 us
    ppermute x1, starting transfers between devices, local(): lax.ppermute(outer, 'narrow', swaps + [(j, i) for i, j in swaps])  4.49 us
    pallas_call x1, Pallas kernels, local(): pl.pallas_call(functools.partial(prepare, levels=levels, rank_k=rank_k),...  2.55 us
  transfers between devices with their start and end apart: 7, of which 0 were waited for; matrix products, arithmetic and copies ran while one was open for 0% of the time, Pallas kernels for 55%

profile of v3, /device:TPU:1, one launch (start us, length us, event | category | flops | bytes accessed | tf_op | source)
XLA Modules:
  0.0 53.7 jit_solution(17610928083278128410)
XLA Ops:
  0.0 2.5 %prepare.1 = (bf16[128,1024]{1,0:T(8,128)(2,1)S(1)}, bf16[128,1024]{1,0:T(8,128)(2,1)S(1)}, f32[128,128]{1,0:T(8,128)S(1)}, f32[4,128,128]{2,1,0:T(8,128)S(1)}, ...) custom-call(s32[1]{0:T(128)} %bitcast.device_ref, s32[4]{0:T(128)} %rank_hbm.3, s32[16,128]{1,0:T(8,128)} %bitcast.5, ...), custom_call_target="tpu_custom_call" | custom-call | flops 1000000000 | bytes 8000000 | tf_op jit(solution)/shard_map/prepare/pallas_call | solution.py:466
  2.6 0.1 collective-permute-start
  2.7 4.5 %collective-permute-start.1 = (bf16[128,1024]{1,0:T(8,128)(2,1)S(1)}, bf16[128,1024]{1,0:T(8,128)(2,1)S(1)}, u32[]{:S(2)}, u32[]{:S(2)}) collective-permute-start(bf16[128,1024]{1,0:T(8,128)(2,1)S(1)} %get-tuple-element.50), channel_id=1, source_target_pairs={{1,2},{3,4},{5,6},{7,8},{9,10},{11,12},{13,14},{2,1},{4,3},{6,5},{... | collective-permute-start | bytes 786440 | tf_op jit(solution)/shard_map/ppermute | solution.py:504
  7.2 0.0 copy-start
  7.2 8.7 %leaf_operators.1 = (bf16[2048,1280]{1,0:T(8,128)(2,1)S(1)}, f8e4m3fn[2048,1280]{1,0:T(32,128)(4,1)S(1)}, bf16[512,2048]{1,0:T(8,128)(2,1)S(1)}, f32[256,256]{1,...) custom-call(s32[4]{0:T(128)} %rank_hbm.3, f32[128,128]{1,0:T(8,128)S(1)} %get-tuple-element.41.cols_ref, ...), custom_call_target="tpu_custom_call" | custom-call | flops 5000000000 | bytes 14000000 | tf_op jit(solution)/shard_map/leaf_operators/pallas_call | solution.py:506
  15.9 0.0 collective-permute-done.inner_ref
  15.9 0.0 collective-permute-done.1.outer_ref
  15.9 0.0 copy-done
  15.9 5.2 %projections.1 = (f32[256,768]{1,0:T(8,128)S(1)}, f32[256,768]{1,0:T(8,128)S(1)}, bf16[1280,1024]{1,0:T(8,128)(2,1)S(1)}, f8e4m3fn[1280,1024]{1,0:T(32,128)(4,1)S(1)}) custom-call(s32[1]{0:T(128)} %bitcast.device_ref, bf16[512,2048]{1,0:T(8,128)(2,1)S(1)} %get-tuple-element.48.w_ref, bf16[2048,1280]{1,0:T(8,128)(2,1)S(1)} %get-tuple-element.46.sh_ref, ...), custom_call_target="tpu_custom_call" | custom-call | flops 5000000000 | bytes 14000000 | tf_op jit(solution)/shard_map/projections/pallas_call | solution.py:529
  21.1 0.1 collective-permute-start.2
  21.2 2.4 %interpolate.2.t0_ref = bf16[512,1024]{1,0:T(8,128)(2,1)S(1)} custom-call(bf16[2048,1280]{1,0:T(8,128)(2,1)S(1)} %get-tuple-element.46.sh_ref, f8e4m3fn[2048,1280]{1,0:T(32,128)(4,1)S(1)} %get-tuple-element.47.s8_ref, bf16[1280,1024]{1,0:T(8,128)(2,1)S(1)} %get-tuple-element.52.m_ref, f8e4m3fn[1280,1024]{1,0:T(32,128)(4,1)S(1)} %get-tuple-element.60.m8_ref), custom_call_target="tpu_custom_call" | custom-call | flops 4000000000 | bytes 8000000 | tf_op jit(solution)/shard_map/interpolate/pallas_call | solution.py:550
  23.6 0.0 collective-permute-done.2.other_ref
  23.6 0.7 %stage.4 = (f32[192,640]{1,0:T(8,128)S(1)}, bf16[192,640]{1,0:T(8,128)(2,1)S(1)}, f32[2,64,512]{2,1,0:T(8,128)S(1)}) custom-call(s32[1]{0:T(128)} %bitcast.device_ref, f32[4,128,128]{2,1,0:T(8,128)S(1)} %get-tuple-element.56.core_ref, f32[256,768]{1,0:T(8,128)S(1)} %get-tuple-element.58.mine_ref, f32[256,768]{1,0:T(8,128)S(1)} %collective-permute-done.2.other_ref), custom_call_target="tpu_custom_call" | custom-call | flops 100000000 | bytes 1000000 | tf_op jit(solution)/shard_map/stage/pallas_call | solution.py:583
  24.3 1.3 %collective-permute-start.3 = (bf16[192,640]{1,0:T(8,128)(2,1)S(1)}, bf16[192,640]{1,0:T(8,128)(2,1)S(1)}, u32[]{:S(2)}, u32[]{:S(2)}) collective-permute-start(bf16[192,640]{1,0:T(8,128)(2,1)S(1)} %get-tuple-element.59), channel_id=1, source_target_pairs={{0,2},{1,3},{2,0},{3,1},{4,6},{5,7},{6,4},{7,5},{8,10},{9,11},{10,... | collective-permute-start | bytes 737288 | tf_op jit(solution)/shard_map/ppermute | solution.py:454
  25.7 6.4 %interpolate.3.t1_ref = bf16[1536,1024]{1,0:T(8,128)(2,1)S(1)} custom-call(bf16[2048,1280]{1,0:T(8,128)(2,1)S(1)} %get-tuple-element.46.sh_ref, f8e4m3fn[2048,1280]{1,0:T(32,128)(4,1)S(1)} %get-tuple-element.47.s8_ref, bf16[1280,1024]{1,0:T(8,128)(2,1)S(1)} %get-tuple-element.52.m_ref, f8e4m3fn[1280,1024]{1,0:T(32,128)(4,1)S(1)} %get-tuple-element.60.m8_ref), custom_call_target="tpu_custom_call" | custom-call | flops 4000000000 | bytes 8000000 | tf_op jit(solution)/shard_map/interpolate/pallas_call | solution.py:550
  32.1 0.0 collective-permute-done.3.other_ref
  32.1 0.6 %stage.5 = (f32[128,640]{1,0:T(8,128)S(1)}, bf16[128,640]{1,0:T(8,128)(2,1)S(1)}, f32[1,64,512]{2,1,0:T(8,128)S(1)}) custom-call(s32[1]{0:T(128)} %bitcast.device_ref, f32[4,128,128]{2,1,0:T(8,128)S(1)} %get-tuple-element.56.core_ref, f32[192,640]{1,0:T(8,128)S(1)} %get-tuple-element.62.mine_ref, bf16[192,640]{1,0:T(8,128)(2,1)S(1)} %collective-permute-done.3.other_ref), custom_call_target="tpu_custom_call" | custom-call | flops 100000000 | bytes 1000000 | tf_op jit(solution)/shard_map/stage/pallas_call | solution.py:583
  32.7 1.5 %collective-permute-start.4 = (bf16[128,640]{1,0:T(8,128)(2,1)S(1)}, bf16[128,640]{1,0:T(8,128)(2,1)S(1)}, u32[]{:S(2)}, u32[]{:S(2)}) collective-permute-start(bf16[128,640]{1,0:T(8,128)(2,1)S(1)} %get-tuple-element.63), channel_id=1, source_target_pairs={{0,4},{1,5},{2,6},{3,7},{4,0},{5,1},{6,2},{7,3},{8,12},{9,13},{10,... | collective-permute-start | bytes 491528 | tf_op jit(solution)/shard_map/ppermute | solution.py:454
  34.2 4.6 %leaf_solve.2.y0_ref = f32[1024,1024]{1,0:T(8,128)S(1)} custom-call(bf16[2048,512]{1,0:T(8,128)(2,1)S(1)} %get-tuple-element.43.a0_ref, bf16[2048,1536]{1,0:T(8,128)(2,1)S(1)} %get-tuple-element.45.a1_ref, bf16[512,1024]{1,0:T(8,128)(2,1)S(1)} %interpolate.2.t0_ref, bf16[1536,1024]{1,0:T(8,128)(2,1)S(1)} %interpolate.3.t1_ref), custom_call_target="tpu_custom_call" | custom-call | flops 4300000256 | bytes 10000000 | tf_op jit(solution)/shard_map/leaf_solve/pallas_call | solution.py:561
  38.8 0.0 collective-permute-done.4.other_ref
  38.8 0.5 stage.6
  39.3 2.4 %collective-permute-start.5 = (bf16[64,512]{1,0:T(8,128)(2,1)S(1)}, bf16[64,512]{1,0:T(8,128)(2,1)S(1)}, u32[]{:S(2)}, u32[]{:S(2)}) collective-permute-start(bf16[64,512]{1,0:T(8,128)(2,1)S(1)} %get-tuple-element.67), channel_id=1, source_target_pairs={{0,8},{1,9},{2,10},{3,11},{4,12},{5,13},{6,14},{7,15},{8,0},{9,1},... | collective-permute-start | bytes 196616 | tf_op jit(solution)/shard_map/ppermute | solution.py:454
  41.7 4.6 %leaf_solve.3.y1_ref = f32[1024,1024]{1,0:T(8,128)S(1)} custom-call(bf16[2048,512]{1,0:T(8,128)(2,1)S(1)} %get-tuple-element.43.a0_ref, bf16[2048,1536]{1,0:T(8,128)(2,1)S(1)} %get-tuple-element.45.a1_ref, bf16[512,1024]{1,0:T(8,128)(2,1)S(1)} %interpolate.2.t0_ref, bf16[1536,1024]{1,0:T(8,128)(2,1)S(1)} %interpolate.3.t1_ref), custom_call_target="tpu_custom_call" | custom-call | flops 4300000256 | bytes 10000000 | tf_op jit(solution)/shard_map/leaf_solve/pallas_call | solution.py:561
  46.3 0.0 collective-permute-done.5.other_ref
  46.3 0.3 stage.7
  46.6 1.6 %collective-permute-start.6 = (f32[256,512]{1,0:T(8,128)S(1)}, f32[256,512]{1,0:T(8,128)S(1)}, u32[]{:S(2)}, u32[]{:S(2)}) collective-permute-start(f32[256,512]{1,0:T(8,128)S(1)} %get-tuple-element.74), channel_id=1, source_target_pairs={{0,1},{1,0},{2,3},{3,2},{4,5},{5,4},{6,7},{7,6},{8,9},{9,8},{10,11... | collective-permute-start | bytes 1572872 | tf_op jit(solution)/shard_map/ppermute | solution.py:454
  48.1 2.7 %update.2.refs_0_ = f32[2048,1024]{1,0:T(8,128)} custom-call(s32[1]{0:T(128)} %bitcast.device_ref, bf16[2048,512]{1,0:T(8,128)(2,1)S(1)} %get-tuple-element.44.left_ref, f32[1024,1024]{1,0:T(8,128)S(1)} %leaf_solve.2.y0_ref, f32[1024,1024]{1,0:T(8,128)S(1)} %leaf_solve.3.y1_ref, f32[256,512]{1,0:T(8,128)S(1)} %get-tuple-element.75.c_ref), custom_call_target="tpu_custom_call" | custom-call | flops 1700000000 | bytes 9000000 | tf_op jit(solution)/shard_map/update/pallas_call | solution.py:624
  50.8 0.0 collective-permute-done.6.c_ref
  50.9 2.7 %update.3 = f32[2048,1024]{1,0:T(8,128)} custom-call(s32[1]{0:T(128)} %bitcast.device_ref, bf16[2048,512]{1,0:T(8,128)(2,1)S(1)} %get-tuple-element.44.left_ref, f32[1024,1024]{1,0:T(8,128)S(1)} %leaf_solve.2.y0_ref, f32[1024,1024]{1,0:T(8,128)S(1)} %leaf_solve.3.y1_ref, ...), custom_call_target="tpu_custom_call", output_to_operand_aliasing={{}: (5, {})} | custom-call | flops 1700000000 | bytes 9000000 | tf_op jit(solution)/shard_map/update/pallas_call | solution.py:624
Async XLA Ops:
  2.6 13.4 %collective-permute-start = (bf16[128,1024]{1,0:T(8,128)(2,1)S(1)}, bf16[128,1024]{1,0:T(8,128)(2,1)S(1)}, u32[]{:S(2)}, u32[]{:S(2)}) collective-permute-start(bf16[128,1024]{1,0:T(8,128)(2,1)S(1)} %get-tuple-element.49), channel_id=1, source_target_pairs={{0,1},{1,0},{2,3},{3,2},{4,5},{5,4},{6,7},{7,6},{8,9},{9,8},{10,11... | collective-permute-start | bytes 786440 | tf_op jit(solution)/shard_map/ppermute | solution.py:454
  2.7 13.3 %collective-permute-start.1 = (bf16[128,1024]{1,0:T(8,128)(2,1)S(1)}, bf16[128,1024]{1,0:T(8,128)(2,1)S(1)}, u32[]{:S(2)}, u32[]{:S(2)}) collective-permute-start(bf16[128,1024]{1,0:T(8,128)(2,1)S(1)} %get-tuple-element.50), channel_id=1, source_target_pairs={{1,2},{3,4},{5,6},{7,8},{9,10},{11,12},{13,14},{2,1},{4,3},{6,5},{... | collective-permute-start | bytes 786440 | tf_op jit(solution)/shard_map/ppermute | solution.py:504
  7.2 8.8 %copy-start = (bf16[1024,1024]{1,0:T(8,128)(2,1)S(1)}, bf16[1024,1024]{1,0:T(8,128)(2,1)}, u32[]{:S(2)}) copy-start(bf16[1024,1024]{1,0:T(8,128)(2,1)} %modes_ref.3) | copy-start | bytes 6291460
  21.1 2.5 %collective-permute-start.2 = (f32[256,768]{1,0:T(8,128)S(1)}, f32[256,768]{1,0:T(8,128)S(1)}, u32[]{:S(2)}, u32[]{:S(2)}) collective-permute-start(f32[256,768]{1,0:T(8,128)S(1)} %get-tuple-element.54), channel_id=1, source_target_pairs={{0,1},{1,0},{2,3},{3,2},{4,5},{5,4},{6,7},{7,6},{8,9},{9,8},{10,11... | collective-permute-start | bytes 2359304 | tf_op jit(solution)/shard_map/ppermute | solution.py:454
  24.3 7.8 %collective-permute-start.3 = (bf16[192,640]{1,0:T(8,128)(2,1)S(1)}, bf16[192,640]{1,0:T(8,128)(2,1)S(1)}, u32[]{:S(2)}, u32[]{:S(2)}) collective-permute-start(bf16[192,640]{1,0:T(8,128)(2,1)S(1)} %get-tuple-element.59), channel_id=1, source_target_pairs={{0,2},{1,3},{2,0},{3,1},{4,6},{5,7},{6,4},{7,5},{8,10},{9,11},{10,... | collective-permute-start | bytes 737288 | tf_op jit(solution)/shard_map/ppermute | solution.py:454
  32.7 6.0 %collective-permute-start.4 = (bf16[128,640]{1,0:T(8,128)(2,1)S(1)}, bf16[128,640]{1,0:T(8,128)(2,1)S(1)}, u32[]{:S(2)}, u32[]{:S(2)}) collective-permute-start(bf16[128,640]{1,0:T(8,128)(2,1)S(1)} %get-tuple-element.63), channel_id=1, source_target_pairs={{0,4},{1,5},{2,6},{3,7},{4,0},{5,1},{6,2},{7,3},{8,12},{9,13},{10,... | collective-permute-start | bytes 491528 | tf_op jit(solution)/shard_map/ppermute | solution.py:454
  39.3 7.0 %collective-permute-start.5 = (bf16[64,512]{1,0:T(8,128)(2,1)S(1)}, bf16[64,512]{1,0:T(8,128)(2,1)S(1)}, u32[]{:S(2)}, u32[]{:S(2)}) collective-permute-start(bf16[64,512]{1,0:T(8,128)(2,1)S(1)} %get-tuple-element.67), channel_id=1, source_target_pairs={{0,8},{1,9},{2,10},{3,11},{4,12},{5,13},{6,14},{7,15},{8,0},{9,1},... | collective-permute-start | bytes 196616 | tf_op jit(solution)/shard_map/ppermute | solution.py:454
  46.6 4.3 %collective-permute-start.6 = (f32[256,512]{1,0:T(8,128)S(1)}, f32[256,512]{1,0:T(8,128)S(1)}, u32[]{:S(2)}, u32[]{:S(2)}) collective-permute-start(f32[256,512]{1,0:T(8,128)S(1)} %get-tuple-element.74), channel_id=1, source_target_pairs={{0,1},{1,0},{2,3},{3,2},{4,5},{5,4},{6,7},{7,6},{8,9},{9,8},{10,11... | collective-permute-start | bytes 1572872 | tf_op jit(solution)/shard_map/ppermute | solution.py:454

commit v4 on v3

--- a/solution.py
+++ b/solution.py
@@ -14,6 +14,7 @@
 F8 = jnp.float8_e4m3fn
 LOW_SCALE = 4096.0
 W8_TOP = 224.0
+W_LOW = 256.0
 TINY = 1e-30
 NOWHERE_BITS = 11
 NOWHERE = 2**NOWHERE_BITS - 1
@@ -292,6 +293,7 @@
     m_ref,
     m8_ref,
     w8_scr,
+    w8_low,
     ws_scr,
     p_scr,
 ):
@@ -307,19 +309,21 @@
     pieces = [slice(first, first + piece) for first in range(0, sh_ref.shape[1], piece)]
 
     def main_part(cols):
-        part = dot(w_ref[...], sh_ref[:, cols])
-        return part[:ranks] + part[ranks:]
+        return dot(w_ref[:ranks, :], sh_ref[:, cols])
 
     parts = [main_part(pieces[0])]
     largest = jnp.max(jnp.abs(w_ref[:ranks, :].astype(F32)), axis=1, keepdims=True)
     largest = jnp.maximum(largest, TINY)
     parts.append(main_part(pieces[1]))
     w8_scr[...] = (w_ref[:ranks, :].astype(F32) * (W8_TOP / largest)).astype(F8)
+    w8_low[...] = (w_ref[ranks:, :].astype(F32) * (W8_TOP * W_LOW / largest)).astype(F8)
     w_back = largest * (1.0 / (W8_TOP * LOW_SCALE))
     for i, cols in enumerate(pieces):
         if i + 2 < len(pieces):
             parts.append(main_part(pieces[i + 2]))
-        part = parts[i] + dot(w8_scr[...], s8_ref[:, cols]) * w_back
+        top = (sh_ref[:, cols] * jnp.asarray(LOW_SCALE / W_LOW, BF16)).astype(F8)
+        part = dot(w8_scr[...], s8_ref[:, cols]) + dot(w8_low[...], top)
+        part = parts[i] + part * w_back
         high, low = split(part)
         ws_scr[:ranks, cols] = high
         ws_scr[ranks:, cols] = low
@@ -335,6 +339,16 @@
     send_ref[:, half:] = h_ref[...]
 
 
+def chunks(rows, lanes, width):
+    across = width // LANES
+    places = [(r, c) for c in range(0, lanes, LANES) for r in range(0, rows, 16)]
+    return [((t // across * 16, t % across * LANES), place) for t, place in enumerate(places)]
+
+
+def chunk_rows(rows, lanes, width):
+    return 16 * -(-(rows // 16) * (lanes // LANES) // (width // LANES))
+
+
 def stage(device_ref, core_ref, mine_ref, other_ref, *refs, level, levels, rank_k, half):
     side = jnp.bitwise_and(lax.shift_right_logical(device_ref[0], level), 1)
     upper = jnp.full((rank_k, half), side, jnp.int32) == 1
@@ -346,18 +360,36 @@
     c_other = jnp.where(upper, coef[rank_k:], coef[:rank_k])
     if level < levels - 1:
         next_ref, send_ref, c_ref = refs[0], refs[1], refs[2]
-        at = half + (levels - 2 - level) * rank_k
-        h_mine = mine_ref[rank_k:, at : at + rank_k]
-        h_other = other_ref[rank_k:, at : at + rank_k].astype(F32)
-        q = mine_ref[rank_k:, :half] + other_ref[rank_k:, :half].astype(F32)
+        at = (levels - 2 - level) * rank_k
+        rows = mine_ref.shape[0]
+        if level == 0:
+            h_all = other_ref[rank_k:, half:]
+        else:
+            columns = {}
+            for (r, c), (_, column) in chunks(rows - rank_k, mine_ref.shape[1] - half, half):
+                piece = other_ref[rows + r : rows + r + 16, c : c + LANES]
+                columns.setdefault(column, []).append(piece)
+            columns = [jnp.concatenate(columns[c], axis=0) for c in sorted(columns)]
+            h_all = jnp.concatenate(columns, axis=1).astype(F32)
+        h_mine = mine_ref[rank_k:, half + at : half + at + rank_k]
+        h_other = h_all[:, at : at + rank_k]
+        q = mine_ref[rank_k:, :half] + other_ref[rank_k:rows, :half].astype(F32)
         q = q - dot_split(h_mine, c_mine) - dot_split(h_other, c_other)
         next_ref[:, :half] = q
-        send_ref[:, :half] = q.astype(send_ref.dtype)
-        end = next_ref.shape[1]
+        after_rows, end = next_ref.shape
+        send_ref[:after_rows, :] = q.astype(send_ref.dtype)
         if end > half:
-            h = mine_ref[rank_k:, half:end] + other_ref[rank_k:, half:end].astype(F32)
+            h = mine_ref[rank_k:, half:end] + h_all[:, : end - half]
             next_ref[:, half:] = h
-            send_ref[:, half:] = h.astype(send_ref.dtype)
+            packed = h[rank_k:].astype(send_ref.dtype)
+            for (r, c), (row, column) in chunks(after_rows - rank_k, end - half, half):
+                piece = packed[row : row + 16, column : column + LANES]
+                send_ref[after_rows + r : after_rows + r + 16, c : c + LANES] = piece
+            filled = (after_rows - rank_k) // 16 * ((end - half) // LANES) % (half // LANES)
+            if filled:
+                rest = send_ref.shape[0] - 16
+                blank = jnp.zeros((16, half - filled * LANES), send_ref.dtype)
+                send_ref[rest:, filled * LANES :] = blank
         c_ref[0] = c_mine
         if level == 0:
             c_ref[1] = c_other
@@ -538,6 +570,7 @@
         ],
         scratch_shapes=[
             pltpu.VMEM((ranks, leaf), F8),
+            pltpu.VMEM((ranks, leaf), F8),
             pltpu.VMEM((2 * ranks, width), BF16),
             pltpu.VMEM((ranks, rhs), F32),
         ],
@@ -576,7 +609,7 @@
             size = (mine.shape[0] - rank_k, half + h_width(level + 1))
             out_shape = [
                 shape(size, F32),
-                shape(size, BF16),
+                shape((size[0] + chunk_rows(size[0] - rank_k, size[1] - half, half), half), BF16),
                 shape((2 if level == 0 else 1, rank_k, half), F32),
             ]
             extra = []

time: 53.9 us -> 53.3 us (0.989)
  no operation moved by 1% of the time
where the time goes in v4:
time: 53.3 us; the launch traced here: 53.1 us
  Pallas kernels  41.7 us (78%)
  starting transfers between devices  11.1 us (21%)
    pallas_call x2, Pallas kernels, run_leaf(): pl.pallas_call(functools.partial(leaf_solve, start=start), in_specs=[whol...  9.12 us
    pallas_call x2, Pallas kernels, run_interpolate(): pl.pallas_call(functools.partial(interpolate, start=start), in_specs=[who...  8.84 us
    pallas_call x1, Pallas kernels, local(): pl.pallas_call(functools.partial(leaf_operators, levels=levels, rank_k=ra...  8.72 us
    ppermute x6, starting transfers between devices, partner(): lax.ppermute(value, 'narrow', [(s, s ^ 1 << bit) for s in range(count)])  6.56 us
    pallas_call x2, Pallas kernels, run_update(): pl.pallas_call(functools.partial(update, own_half=own_half), in_specs=[sc...  5.45 us
    pallas_call x1, Pallas kernels, local(): pl.pallas_call(projections, in_specs=[scalars()] + [whole()] * 7, out_spe...  4.92 us
    ppermute x1, starting transfers between devices, local(): lax.ppermute(outer, 'narrow', swaps + [(j, i) for i, j in swaps])  4.49 us
    pallas_call x1, Pallas kernels, local(): pl.pallas_call(functools.partial(prepare, levels=levels, rank_k=rank_k),...  2.55 us
  transfers between devices with their start and end apart: 7, of which 0 were waited for; matrix products, arithmetic and copies ran while one was open for 0% of the time, Pallas kernels for 55%

profile of v4, /device:TPU:1, one launch (start us, length us, event | category | flops | bytes accessed | tf_op | source)
XLA Modules:
  0.0 53.1 jit_solution(1272236630228301133)
XLA Ops:
  0.0 2.5 %prepare.1 = (bf16[128,1024]{1,0:T(8,128)(2,1)S(1)}, bf16[128,1024]{1,0:T(8,128)(2,1)S(1)}, f32[128,128]{1,0:T(8,128)S(1)}, f32[4,128,128]{2,1,0:T(8,128)S(1)}, ...) custom-call(s32[1]{0:T(128)} %bitcast.device_ref, s32[4]{0:T(128)} %rank_hbm.3, s32[16,128]{1,0:T(8,128)} %bitcast.5, ...), custom_call_target="tpu_custom_call" | custom-call | flops 1000000000 | bytes 8000000 | tf_op jit(solution)/shard_map/prepare/pallas_call | solution.py:498
  2.6 0.1 collective-permute-start
  2.7 4.5 %collective-permute-start.1 = (bf16[128,1024]{1,0:T(8,128)(2,1)S(1)}, bf16[128,1024]{1,0:T(8,128)(2,1)S(1)}, u32[]{:S(2)}, u32[]{:S(2)}) collective-permute-start(bf16[128,1024]{1,0:T(8,128)(2,1)S(1)} %get-tuple-element.50), channel_id=1, source_target_pairs={{1,2},{3,4},{5,6},{7,8},{9,10},{11,12},{13,14},{2,1},{4,3},{6,5},{... | collective-permute-start | bytes 786440 | tf_op jit(solution)/shard_map/ppermute | solution.py:536
  7.2 0.0 copy-start
  7.2 8.7 %leaf_operators.1 = (bf16[2048,1280]{1,0:T(8,128)(2,1)S(1)}, f8e4m3fn[2048,1280]{1,0:T(32,128)(4,1)S(1)}, bf16[512,2048]{1,0:T(8,128)(2,1)S(1)}, f32[256,256]{1,...) custom-call(s32[4]{0:T(128)} %rank_hbm.3, f32[128,128]{1,0:T(8,128)S(1)} %get-tuple-element.41.cols_ref, ...), custom_call_target="tpu_custom_call" | custom-call | flops 5000000000 | bytes 14000000 | tf_op jit(solution)/shard_map/leaf_operators/pallas_call | solution.py:538
  15.9 0.0 collective-permute-done.inner_ref
  15.9 0.0 collective-permute-done.1.outer_ref
  15.9 0.0 copy-done
  15.9 4.9 %projections.1 = (f32[256,768]{1,0:T(8,128)S(1)}, f32[256,768]{1,0:T(8,128)S(1)}, bf16[1280,1024]{1,0:T(8,128)(2,1)S(1)}, f8e4m3fn[1280,1024]{1,0:T(32,128)(4,1)S(1)}) custom-call(s32[1]{0:T(128)} %bitcast.device_ref, bf16[512,2048]{1,0:T(8,128)(2,1)S(1)} %get-tuple-element.48.w_ref, bf16[2048,1280]{1,0:T(8,128)(2,1)S(1)} %get-tuple-element.46.sh_ref, ...), custom_call_target="tpu_custom_call" | custom-call | flops 5000000000 | bytes 14000000 | tf_op jit(solution)/shard_map/projections/pallas_call | solution.py:561
  20.9 0.1 collective-permute-start.2
  20.9 2.4 %interpolate.2.t0_ref = bf16[512,1024]{1,0:T(8,128)(2,1)S(1)} custom-call(bf16[2048,1280]{1,0:T(8,128)(2,1)S(1)} %get-tuple-element.46.sh_ref, f8e4m3fn[2048,1280]{1,0:T(32,128)(4,1)S(1)} %get-tuple-element.47.s8_ref, bf16[1280,1024]{1,0:T(8,128)(2,1)S(1)} %get-tuple-element.52.m_ref, f8e4m3fn[1280,1024]{1,0:T(32,128)(4,1)S(1)} %get-tuple-element.60.m8_ref), custom_call_target="tpu_custom_call" | custom-call | flops 4000000000 | bytes 8000000 | tf_op jit(solution)/shard_map/interpolate/pallas_call | solution.py:583
  23.4 0.0 collective-permute-done.2.other_ref
  23.4 0.7 %stage.4 = (f32[192,640]{1,0:T(8,128)S(1)}, bf16[224,512]{1,0:T(8,128)(2,1)S(1)}, f32[2,64,512]{2,1,0:T(8,128)S(1)}) custom-call(s32[1]{0:T(128)} %bitcast.device_ref, f32[4,128,128]{2,1,0:T(8,128)S(1)} %get-tuple-element.56.core_ref, f32[256,768]{1,0:T(8,128)S(1)} %get-tuple-element.58.mine_ref, f32[256,768]{1,0:T(8,128)S(1)} %collective-permute-done.2.other_ref), custom_call_target="tpu_custom_call" | custom-call | flops 100000000 | bytes 1000000 | tf_op jit(solution)/shard_map/stage/pallas_call | solution.py:616
  24.1 1.3 %collective-permute-start.3 = (bf16[224,512]{1,0:T(8,128)(2,1)S(1)}, bf16[224,512]{1,0:T(8,128)(2,1)S(1)}, u32[]{:S(2)}, u32[]{:S(2)}) collective-permute-start(bf16[224,512]{1,0:T(8,128)(2,1)S(1)} %get-tuple-element.59), channel_id=1, source_target_pairs={{0,2},{1,3},{2,0},{3,1},{4,6},{5,7},{6,4},{7,5},{8,10},{9,11},{10,... | collective-permute-start | bytes 688136 | tf_op jit(solution)/shard_map/ppermute | solution.py:486
  25.4 6.4 %interpolate.3.t1_ref = bf16[1536,1024]{1,0:T(8,128)(2,1)S(1)} custom-call(bf16[2048,1280]{1,0:T(8,128)(2,1)S(1)} %get-tuple-element.46.sh_ref, f8e4m3fn[2048,1280]{1,0:T(32,128)(4,1)S(1)} %get-tuple-element.47.s8_ref, bf16[1280,1024]{1,0:T(8,128)(2,1)S(1)} %get-tuple-element.52.m_ref, f8e4m3fn[1280,1024]{1,0:T(32,128)(4,1)S(1)} %get-tuple-element.60.m8_ref), custom_call_target="tpu_custom_call" | custom-call | flops 4000000000 | bytes 8000000 | tf_op jit(solution)/shard_map/interpolate/pallas_call | solution.py:583
  31.9 0.0 collective-permute-done.3.other_ref
  31.9 0.6 %stage.5 = (f32[128,640]{1,0:T(8,128)S(1)}, bf16[144,512]{1,0:T(8,128)(2,1)S(1)}, f32[1,64,512]{2,1,0:T(8,128)S(1)}) custom-call(s32[1]{0:T(128)} %bitcast.device_ref, f32[4,128,128]{2,1,0:T(8,128)S(1)} %get-tuple-element.56.core_ref, f32[192,640]{1,0:T(8,128)S(1)} %get-tuple-element.62.mine_ref, bf16[224,512]{1,0:T(8,128)(2,1)S(1)} %collective-permute-done.3.other_ref), custom_call_target="tpu_custom_call" | custom-call | flops 100000000 | bytes 1000000 | tf_op jit(solution)/shard_map/stage/pallas_call | solution.py:616
  32.5 1.3 %collective-permute-start.4 = (bf16[144,512]{1,0:T(8,128)(2,1)S(1)}, bf16[144,512]{1,0:T(8,128)(2,1)S(1)}, u32[]{:S(2)}, u32[]{:S(2)}) collective-permute-start(bf16[144,512]{1,0:T(8,128)(2,1)S(1)} %get-tuple-element.63), channel_id=1, source_target_pairs={{0,4},{1,5},{2,6},{3,7},{4,0},{5,1},{6,2},{7,3},{8,12},{9,13},{10,... | collective-permute-start | bytes 442376 | tf_op jit(solution)/shard_map/ppermute | solution.py:486
  33.9 4.6 %leaf_solve.2.y0_ref = f32[1024,1024]{1,0:T(8,128)S(1)} custom-call(bf16[2048,512]{1,0:T(8,128)(2,1)S(1)} %get-tuple-element.43.a0_ref, bf16[2048,1536]{1,0:T(8,128)(2,1)S(1)} %get-tuple-element.45.a1_ref, bf16[512,1024]{1,0:T(8,128)(2,1)S(1)} %interpolate.2.t0_ref, bf16[1536,1024]{1,0:T(8,128)(2,1)S(1)} %interpolate.3.t1_ref), custom_call_target="tpu_custom_call" | custom-call | flops 4300000256 | bytes 10000000 | tf_op jit(solution)/shard_map/leaf_solve/pallas_call | solution.py:594
  38.4 0.0 collective-permute-done.4.other_ref
  38.4 0.5 stage.6
  38.9 2.1 %collective-permute-start.5 = (bf16[64,512]{1,0:T(8,128)(2,1)S(1)}, bf16[64,512]{1,0:T(8,128)(2,1)S(1)}, u32[]{:S(2)}, u32[]{:S(2)}) collective-permute-start(bf16[64,512]{1,0:T(8,128)(2,1)S(1)} %get-tuple-element.67), channel_id=1, source_target_pairs={{0,8},{1,9},{2,10},{3,11},{4,12},{5,13},{6,14},{7,15},{8,0},{9,1},... | collective-permute-start | bytes 196616 | tf_op jit(solution)/shard_map/ppermute | solution.py:486
  41.1 4.6 %leaf_solve.3.y1_ref = f32[1024,1024]{1,0:T(8,128)S(1)} custom-call(bf16[2048,512]{1,0:T(8,128)(2,1)S(1)} %get-tuple-element.43.a0_ref, bf16[2048,1536]{1,0:T(8,128)(2,1)S(1)} %get-tuple-element.45.a1_ref, bf16[512,1024]{1,0:T(8,128)(2,1)S(1)} %interpolate.2.t0_ref, bf16[1536,1024]{1,0:T(8,128)(2,1)S(1)} %interpolate.3.t1_ref), custom_call_target="tpu_custom_call" | custom-call | flops 4300000256 | bytes 10000000 | tf_op jit(solution)/shard_map/leaf_solve/pallas_call | solution.py:594
  45.6 0.0 collective-permute-done.5.other_ref
  45.6 0.3 stage.7
  45.9 1.6 %collective-permute-start.6 = (f32[256,512]{1,0:T(8,128)S(1)}, f32[256,512]{1,0:T(8,128)S(1)}, u32[]{:S(2)}, u32[]{:S(2)}) collective-permute-start(f32[256,512]{1,0:T(8,128)S(1)} %get-tuple-element.74), channel_id=1, source_target_pairs={{0,1},{1,0},{2,3},{3,2},{4,5},{5,4},{6,7},{7,6},{8,9},{9,8},{10,11... | collective-permute-start | bytes 1572872 | tf_op jit(solution)/shard_map/ppermute | solution.py:486
  47.5 2.7 %update.2.refs_0_ = f32[2048,1024]{1,0:T(8,128)} custom-call(s32[1]{0:T(128)} %bitcast.device_ref, bf16[2048,512]{1,0:T(8,128)(2,1)S(1)} %get-tuple-element.44.left_ref, f32[1024,1024]{1,0:T(8,128)S(1)} %leaf_solve.2.y0_ref, f32[1024,1024]{1,0:T(8,128)S(1)} %leaf_solve.3.y1_ref, f32[256,512]{1,0:T(8,128)S(1)} %get-tuple-element.75.c_ref), custom_call_target="tpu_custom_call" | custom-call | flops 1700000000 | bytes 9000000 | tf_op jit(solution)/shard_map/update/pallas_call | solution.py:657
  50.2 0.0 collective-permute-done.6.c_ref
  50.3 2.7 %update.3 = f32[2048,1024]{1,0:T(8,128)} custom-call(s32[1]{0:T(128)} %bitcast.device_ref, bf16[2048,512]{1,0:T(8,128)(2,1)S(1)} %get-tuple-element.44.left_ref, f32[1024,1024]{1,0:T(8,128)S(1)} %leaf_solve.2.y0_ref, f32[1024,1024]{1,0:T(8,128)S(1)} %leaf_solve.3.y1_ref, ...), custom_call_target="tpu_custom_call", output_to_operand_aliasing={{}: (5, {})} | custom-call | flops 1700000000 | bytes 9000000 | tf_op jit(solution)/shard_map/update/pallas_call | solution.py:657
Async XLA Ops:
  2.6 13.4 %collective-permute-start = (bf16[128,1024]{1,0:T(8,128)(2,1)S(1)}, bf16[128,1024]{1,0:T(8,128)(2,1)S(1)}, u32[]{:S(2)}, u32[]{:S(2)}) collective-permute-start(bf16[128,1024]{1,0:T(8,128)(2,1)S(1)} %get-tuple-element.49), channel_id=1, source_target_pairs={{0,1},{1,0},{2,3},{3,2},{4,5},{5,4},{6,7},{7,6},{8,9},{9,8},{10,11... | collective-permute-start | bytes 786440 | tf_op jit(solution)/shard_map/ppermute | solution.py:486
  2.7 13.3 %collective-permute-start.1 = (bf16[128,1024]{1,0:T(8,128)(2,1)S(1)}, bf16[128,1024]{1,0:T(8,128)(2,1)S(1)}, u32[]{:S(2)}, u32[]{:S(2)}) collective-permute-start(bf16[128,1024]{1,0:T(8,128)(2,1)S(1)} %get-tuple-element.50), channel_id=1, source_target_pairs={{1,2},{3,4},{5,6},{7,8},{9,10},{11,12},{13,14},{2,1},{4,3},{6,5},{... | collective-permute-start | bytes 786440 | tf_op jit(solution)/shard_map/ppermute | solution.py:536
  7.2 8.8 %copy-start = (bf16[1024,1024]{1,0:T(8,128)(2,1)S(1)}, bf16[1024,1024]{1,0:T(8,128)(2,1)}, u32[]{:S(2)}) copy-start(bf16[1024,1024]{1,0:T(8,128)(2,1)} %modes_ref.3) | copy-start | bytes 6291460
  20.9 2.5 %collective-permute-start.2 = (f32[256,768]{1,0:T(8,128)S(1)}, f32[256,768]{1,0:T(8,128)S(1)}, u32[]{:S(2)}, u32[]{:S(2)}) collective-permute-start(f32[256,768]{1,0:T(8,128)S(1)} %get-tuple-element.54), channel_id=1, source_target_pairs={{0,1},{1,0},{2,3},{3,2},{4,5},{5,4},{6,7},{7,6},{8,9},{9,8},{10,11... | collective-permute-start | bytes 2359304 | tf_op jit(solution)/shard_map/ppermute | solution.py:486
  24.1 7.8 %collective-permute-start.3 = (bf16[224,512]{1,0:T(8,128)(2,1)S(1)}, bf16[224,512]{1,0:T(8,128)(2,1)S(1)}, u32[]{:S(2)}, u32[]{:S(2)}) collective-permute-start(bf16[224,512]{1,0:T(8,128)(2,1)S(1)} %get-tuple-element.59), channel_id=1, source_target_pairs={{0,2},{1,3},{2,0},{3,1},{4,6},{5,7},{6,4},{7,5},{8,10},{9,11},{10,... | collective-permute-start | bytes 688136 | tf_op jit(solution)/shard_map/ppermute | solution.py:486
  32.5 5.9 %collective-permute-start.4 = (bf16[144,512]{1,0:T(8,128)(2,1)S(1)}, bf16[144,512]{1,0:T(8,128)(2,1)S(1)}, u32[]{:S(2)}, u32[]{:S(2)}) collective-permute-start(bf16[144,512]{1,0:T(8,128)(2,1)S(1)} %get-tuple-element.63), channel_id=1, source_target_pairs={{0,4},{1,5},{2,6},{3,7},{4,0},{5,1},{6,2},{7,3},{8,12},{9,13},{10,... | collective-permute-start | bytes 442376 | tf_op jit(solution)/shard_map/ppermute | solution.py:486
  38.9 6.7 %collective-permute-start.5 = (bf16[64,512]{1,0:T(8,128)(2,1)S(1)}, bf16[64,512]{1,0:T(8,128)(2,1)S(1)}, u32[]{:S(2)}, u32[]{:S(2)}) collective-permute-start(bf16[64,512]{1,0:T(8,128)(2,1)S(1)} %get-tuple-element.67), channel_id=1, source_target_pairs={{0,8},{1,9},{2,10},{3,11},{4,12},{5,13},{6,14},{7,15},{8,0},{9,1},... | collective-permute-start | bytes 196616 | tf_op jit(solution)/shard_map/ppermute | solution.py:486
  45.9 4.3 %collective-permute-start.6 = (f32[256,512]{1,0:T(8,128)S(1)}, f32[256,512]{1,0:T(8,128)S(1)}, u32[]{:S(2)}, u32[]{:S(2)}) collective-permute-start(f32[256,512]{1,0:T(8,128)S(1)} %get-tuple-element.74), channel_id=1, source_target_pairs={{0,1},{1,0},{2,3},{3,2},{4,5},{5,4},{6,7},{7,6},{8,9},{9,8},{10,11... | collective-permute-start | bytes 1572872 | tf_op jit(solution)/shard_map/ppermute | solution.py:486
